TPU v7x, 512 devices: a whole 4x8x8 slice. The times are simulated.
512 devices in a mesh: st: 128 (over z, y, core), hd: 4 (over x).
Axes of the slice: x: 4, y: 8, z: 8, core: 2. Of those that a mesh axis runs over, the one named last changes fastest.
Arguments:
- event_queries: bfloat16 [65536, 1024], P('st', 'hd'), may hold values from -10 to 10
- event_values: bfloat16 [65536, 1024], P('st', 'hd'), may hold values from -64 to 64
- frame_keys: bfloat16 [65536, 1024], P('st', 'hd'), may hold values from -10 to 10
- frame_values: bfloat16 [65536, 1024], P('st', 'hd'), may hold values from -64 to 64
- partner: int32 [256, 3], P('st'), may hold values from 0 to 255, as said below
- live_count: int32 [256], P('st'), may hold values from 1 to 3
- event_cotangent: bfloat16 [65536, 1024], P('st', 'hd'), may hold values from -6 to 6
- frame_cotangent: bfloat16 [65536, 1024], P('st', 'hd'), may hold values from -6 to 6
Outputs:
- event_out: bfloat16 [65536, 1024], P('st', 'hd')
- frame_out: bfloat16 [65536, 1024], P('st', 'hd')
- grad_queries: bfloat16 [65536, 1024], P('st', 'hd')
- grad_event_values: bfloat16 [65536, 1024], P('st', 'hd')
- grad_keys: bfloat16 [65536, 1024], P('st', 'hd')
- grad_frame_values: bfloat16 [65536, 1024], P('st', 'hd')
Inputs may be any that keep to these rules, and one draw needn't show every extreme that they name: `partner`: slot 0 of event block a is frame block a; the live slots of a name distinct frame blocks f with f // 2 between a // 2 - 1 and a // 2 + 1; the other slots hold a.
All inputs are finite; a program needn't handle non-finite values.
Results may differ from a plain program's by a relative error of at most 0.022.
Values may be sent and summed in bfloat16 or wider, within the bound.
No kernel may reach another device: no remote copies, remote signals or barrier semaphores. Data moves between devices by JAX's collectives and lax.ppermute only.
A program may use at most 64 MiB of HBM per device.

v0:
```python
import jax
import jax.numpy as jnp
from jax import lax
from jax.sharding import PartitionSpec as P

DH = 64
BLOCK = 256
SLOTS = 3


NEG = -1e30
EPS = 1e-06


def extended(cells, sides, width):
    for axis, dim in sides:
        count = lax.axis_size(axis)
        ends = count - 1
        head = lax.slice_in_dim(cells, 0, width, axis=dim)
        tail = lax.slice_in_dim(cells, cells.shape[dim] - width, cells.shape[dim], axis=dim)
        cells = jnp.concatenate(
            [
                lax.ppermute(tail, axis, [(i, (i + 1) % count) for i in range(ends)]),
                cells,
                lax.ppermute(head, axis, [((i + 1) % count, i) for i in range(ends)]),
            ],
            axis=dim,
        )
    return cells


def shifted(value, axis, steps):
    count = lax.axis_size(axis)
    first, last = (max(0, -steps), min(count, count - steps))
    return lax.ppermute(value, axis, [(source, source + steps) for source in range(first, last)])


def head_probs(scores, live_slots):
    masked = jnp.where(live_slots[None, :, None], scores, NEG)
    top = jnp.max(masked, axis=(1, 2), keepdims=True)
    expo = jnp.exp(masked - top)
    return expo / jnp.sum(expo, axis=(1, 2), keepdims=True)


def merge_columns(tops, sums):
    top = jnp.maximum(jnp.maximum(tops[0], tops[1]), tops[2])
    ratios = [jnp.exp(value - top) for value in tops]
    total = ratios[0] * sums[0] + ratios[1] * sums[1] + ratios[2] * sums[2]
    return (top, total, ratios)


def heads_first(values):
    return jnp.transpose(values, (1, 0, 2))


def slots_heads_first(values):
    return jnp.transpose(values, (2, 0, 1, 3))


def on_device(
    event_queries,
    event_values,
    frame_keys,
    frame_values,
    partner,
    live_count,
    event_cotangent,
    frame_cotangent,
):
    block_count = partner.shape[0]
    rows, features = event_queries.shape
    heads = features // DH
    width = features * lax.axis_size("hd")
    scale = DH ** (-0.5)
    runs = lax.axis_size("st")
    place = lax.axis_index("st")
    window_slot = partner - (place - 1) * block_count
    live = jnp.arange(SLOTS)[None, :] < live_count[:, None]
    chosen = (window_slot[:, :, None] == jnp.arange(3 * block_count)[None, None, :]) & live[
        :, :, None
    ]
    select = chosen.astype(jnp.float32)
    chosen_tiles = chosen[:, :, :, None, None]

    def blocks(values):
        return values.reshape(-1, BLOCK, heads, DH)

    def flatten(values):
        return values.reshape(-1, features)

    def middle(window):
        return window[block_count : 2 * block_count]

    def outer(window, offset):
        low = (offset + 1) * block_count
        return window[low : low + block_count]

    query_blocks = blocks(event_queries)
    value_blocks = blocks(event_values)
    fetched = extended(jnp.stack((frame_keys, frame_values)), (("st", 1),), rows)
    pair_window = fetched.reshape(2, 3 * block_count, BLOCK, heads, DH)

    def forward_block(item):
        queries, values, slots, live_slots = item

        def forward_head(head_item):
            head_q, head_v, head_k, head_fv = head_item
            scores = scale * jnp.einsum(
                "id,sjd->isj", head_q, head_k, preferred_element_type=jnp.float32
            )
            weights = head_probs(scores, live_slots).astype(jnp.bfloat16)
            attended = jnp.einsum(
                "isj,sjd->id", weights, head_fv, preferred_element_type=jnp.float32
            )
            top = jnp.max(scores, axis=0)
            expo = jnp.exp(scores - top[None])
            tile_acc = jnp.einsum(
                "isj,id->sjd", expo.astype(jnp.bfloat16), head_v, preferred_element_type=jnp.float32
            )
            return (attended, top, jnp.sum(expo, axis=0), tile_acc)

        attended, top, total, tile_acc = lax.map(
            forward_head,
            (
                heads_first(queries),
                heads_first(values),
                slots_heads_first(pair_window[0][slots]),
                slots_heads_first(pair_window[1][slots]),
            ),
        )
        return (
            jnp.transpose(attended, (1, 0, 2)),
            jnp.transpose(top, (1, 0, 2)),
            jnp.transpose(total, (1, 0, 2)),
            jnp.transpose(tile_acc, (1, 2, 0, 3)),
        )

    event_att, tile_top, tile_sum, tile_acc = lax.map(
        forward_block, (query_blocks, value_blocks, window_slot, live)
    )
    top_win = jnp.max(jnp.where(chosen_tiles, tile_top[:, :, None], NEG), axis=(0, 1))
    gap = jnp.where(
        chosen_tiles, jnp.exp(jnp.minimum(tile_top[:, :, None] - top_win[None, None], 0.0)), 0.0
    )
    sum_win = jnp.sum(gap * tile_sum[:, :, None], axis=(0, 1))
    tops = [middle(top_win)]
    sums = [middle(sum_win)]
    for offset in (-1, 1):
        got = shifted((outer(top_win, offset), outer(sum_win, offset)), "st", offset)
        source = place - offset
        tops.append(jnp.where((source >= 0) & (source < runs), got[0], NEG))
        sums.append(got[1])
    col_max, col_total, ratios = merge_columns(tops, sums)
    spread = extended(jnp.stack((col_max, col_total)), (("st", 1),), block_count)
    factor = jnp.where(
        live[:, :, None, None],
        jnp.exp(tile_top - spread[0][window_slot]) / spread[1][window_slot],
        0.0,
    )
    weighted = tile_acc * jnp.transpose(factor, (0, 1, 3, 2))[:, :, :, :, None]
    tile_win = jnp.einsum("tsw,tsjhd->wjhd", select, weighted, precision=lax.Precision.HIGHEST)
    frame_att = middle(tile_win)
    for offset in (-1, 1):
        frame_att = frame_att + blocks(shifted(flatten(outer(tile_win, offset)), "st", offset))
    event_flat = flatten(event_att)
    frame_flat = flatten(frame_att)
    squares = lax.psum(
        (jnp.sum(event_flat * event_flat, axis=1), jnp.sum(frame_flat * frame_flat, axis=1)), "hd"
    )
    event_rms = lax.rsqrt(squares[0] / width + EPS)[:, None]
    frame_rms = lax.rsqrt(squares[1] / width + EPS)[:, None]
    event_normed = event_flat * event_rms
    frame_normed = frame_flat * frame_rms
    event_out = event_normed.astype(jnp.bfloat16)
    frame_out = frame_normed.astype(jnp.bfloat16)
    event_cot = event_cotangent.astype(jnp.float32)
    frame_cot = frame_cotangent.astype(jnp.float32)
    slopes = lax.psum(
        (jnp.sum(event_cot * event_normed, axis=1), jnp.sum(frame_cot * frame_normed, axis=1)), "hd"
    )
    event_grad = (event_rms * (event_cot - event_normed * (slopes[0] / width)[:, None])).astype(
        jnp.bfloat16
    )
    frame_grad = (frame_rms * (frame_cot - frame_normed * (slopes[1] / width)[:, None])).astype(
        jnp.bfloat16
    )
    event_delta = jnp.sum(blocks(event_grad.astype(jnp.float32) * event_flat), axis=3)
    frame_delta = jnp.transpose(
        jnp.sum(blocks(frame_grad.astype(jnp.float32) * frame_flat), axis=3), (0, 2, 1)
    )
    stats_win = extended(jnp.stack((col_max, col_total, frame_delta)), (("st", 1),), block_count)
    cot_win = extended(frame_grad, (("st", 0),), rows)
    key_win = pair_window[0]
    val_win = pair_window[1]
    grad_win = cot_win.reshape(3 * block_count, BLOCK, heads, DH)

    def backward_block(item):
        queries, values, grads, delta, slots, live_slots = item

        def backward_head(head_item):
            (
                head_q,
                head_v,
                head_g,
                head_delta,
                head_k,
                head_fv,
                head_fg,
                col_top,
                col_sum,
                col_delta,
            ) = head_item
            scores = scale * jnp.einsum(
                "id,sjd->isj", head_q, head_k, preferred_element_type=jnp.float32
            )
            row_p = head_probs(scores, live_slots)
            col_p = jnp.where(
                live_slots[None, :, None], jnp.exp(scores - col_top[None]) / col_sum[None], 0.0
            )
            row_change = jnp.einsum(
                "id,sjd->isj", head_g, head_fv, preferred_element_type=jnp.float32
            )
            col_change = jnp.einsum(
                "id,sjd->isj", head_v, head_fg, preferred_element_type=jnp.float32
            )
            slope = (
                scale
                * (
                    row_p * (row_change - head_delta[:, None, None])
                    + col_p * (col_change - col_delta[None])
                )
            ).astype(jnp.bfloat16)
            grad_q = jnp.einsum(
                "isj,sjd->id", slope, head_k, preferred_element_type=jnp.float32
            ).astype(jnp.bfloat16)
            grad_v = jnp.einsum(
                "isj,sjd->id",
                col_p.astype(jnp.bfloat16),
                head_fg,
                preferred_element_type=jnp.float32,
            ).astype(jnp.bfloat16)
            key_part = jnp.einsum("isj,id->sjd", slope, head_q, preferred_element_type=jnp.float32)
            value_part = jnp.einsum(
                "isj,id->sjd",
                row_p.astype(jnp.bfloat16),
                head_g,
                preferred_element_type=jnp.float32,
            )
            return (grad_q, grad_v, key_part, value_part)

        grad_q, grad_v, key_part, value_part = lax.map(
            backward_head,
            (
                heads_first(queries),
                heads_first(values),
                heads_first(grads),
                jnp.transpose(delta),
                slots_heads_first(key_win[slots]),
                slots_heads_first(val_win[slots]),
                slots_heads_first(grad_win[slots]),
                heads_first(stats_win[0][slots]),
                heads_first(stats_win[1][slots]),
                heads_first(stats_win[2][slots]),
            ),
        )
        return (
            jnp.transpose(grad_q, (1, 0, 2)),
            jnp.transpose(grad_v, (1, 0, 2)),
            jnp.transpose(key_part, (1, 2, 0, 3)),
            jnp.transpose(value_part, (1, 2, 0, 3)),
        )

    grad_q, grad_v, key_parts, value_parts = lax.map(
        backward_block,
        (query_blocks, value_blocks, blocks(event_grad), event_delta, window_slot, live),
    )
    key_back = jnp.einsum("tsw,tsjhd->wjhd", select, key_parts, precision=lax.Precision.HIGHEST)
    value_back = jnp.einsum("tsw,tsjhd->wjhd", select, value_parts, precision=lax.Precision.HIGHEST)
    back = jnp.stack((key_back.reshape(-1, features), value_back.reshape(-1, features)))
    total = back[:, rows : 2 * rows]
    for offset in (-1, 1):
        low = (offset + 1) * rows
        sent = back[:, low : low + rows].astype(jnp.bfloat16)
        total = total + shifted(sent, "st", offset).astype(jnp.float32)
    grad_queries = flatten(grad_q)
    grad_event_values = flatten(grad_v)
    grad_keys = total[0].astype(jnp.bfloat16)
    grad_frame_values = total[1].astype(jnp.bfloat16)
    return (event_out, frame_out, grad_queries, grad_event_values, grad_keys, grad_frame_values)


def solution(mesh):
    in_specs = (
        P("st", "hd"),
        P("st", "hd"),
        P("st", "hd"),
        P("st", "hd"),
        P("st", None),
        P("st"),
        P("st", "hd"),
        P("st", "hd"),
    )
    out_specs = (
        P("st", "hd"),
        P("st", "hd"),
        P("st", "hd"),
        P("st", "hd"),
        P("st", "hd"),
        P("st", "hd"),
    )
    return jax.shard_map(
        on_device, mesh=mesh, in_specs=in_specs, out_specs=out_specs, check_vma=False
    )
```

profile of v0, /device:TPU:258, one launch (start us, length us, event | category | flops | bytes accessed | tf_op | source)
XLA Modules:
  0.0 304.5 jit_solution(18117212062722882589)
XLA Ops:
  1.8 1.9 collective-permute-start
  3.7 7.0 %collective-permute-start.1 = (bf16[2,512,256]{2,1,0:T(8,128)(2,1)S(1)}, bf16[2,512,256]{2,1,0:T(8,128)(2,1)S(1)}, u32[]{:S(2)}, u32[]{:S(2)}) collective-permute-start(bf16[2,512,256]{2,1,0:T(8,128)(2,1)S(1)} %pad_maximum_fusion.2), channel_id=1, source_target_pairs={{4,0},{8,4},{12,8},{16,12},{20,16},{24,20},{28,24},{32,28},{36,32}... | collective-permute-start | bytes 1572872 | tf_op jit(solution)/shard_map/ppermute | solution.py:25
  11.4 1.3 reshape.299
  15.6 1.7 collective-permute-done.1
  17.5 2.9 reshape.293
  20.4 4.1 %copy.207 = bf16[2,6,256,4,64]{2,4,3,1,0:T(8,128)(2,1)S(1)} copy(bf16[2,6,256,4,64]{4,3,2,1,0:T(4,128)(2,1)} %reshape.293) | data formatting | bytes 3145728 | tf_op jit(solution)/shard_map/while | solution.py:138
  24.5 1.3 broadcast.141.clone
  25.8 26.9 %while.71 = (s32[]{:T(128)}, f32[2,256,4,64]{1,3,2,0:T(8,128)}, f32[2,3,4,256]{3,2,1,0:T(4,128)}, f32[2,3,4,256]{3,2,1,0:T(4,128)}, f32[2,3,256,4,64]{2,4,1,3,0:...) while((s32[]{:T(128)}, f32[2,256,4,64]{1,3,2,0:T(8,128)}, ...), condition=%wide.region_7.8_spmd.clone, body=%wide.region_0.7_spmd.sunk.clone | while | flops 78445576 | bytes 15699019 | solution.py:138
  28.2 8.1 %while.70 = (s32[]{:T(128)}, f32[4,256,64]{1,2,0:T(8,128)}, f32[4,3,256]{2,1,0:T(4,128)S(1)}, f32[4,3,256]{2,1,0:T(4,128)S(1)}, f32[4,3,256,64]{2,3,1,0:T(8,128)...) while((s32[]{:T(128)}, f32[4,256,64]{1,2,0:T(8,128)}, ...), condition=%wide.region_6.6_spmd, body=%wide.region_1.5_spmd.sunk | while | flops 78444544 | bytes 3709044 | solution.py:122
  41.6 8.1 %while.70 = (s32[]{:T(128)}, f32[4,256,64]{1,2,0:T(8,128)}, f32[4,3,256]{2,1,0:T(4,128)S(1)}, f32[4,3,256]{2,1,0:T(4,128)S(1)}, f32[4,3,256,64]{2,3,1,0:T(8,128)...) while((s32[]{:T(128)}, f32[4,256,64]{1,2,0:T(8,128)}, ...), condition=%wide.region_6.6_spmd, body=%wide.region_1.5_spmd.sunk | while | flops 78444544 | bytes 3709044 | solution.py:122
  54.5 7.1 %collective-permute-start.4 = (f32[2,4,256]{2,1,0:T(4,128)S(1)}, f32[2,4,256]{2,1,0:T(4,128)S(1)}, u32[]{:S(2)}, u32[]{:S(2)}) collective-permute-start(f32[2,4,256]{2,1,0:T(4,128)S(1)} %get-tuple-element.684), channel_id=1, source_target_pairs={{4,0},{8,4},{12,8},{16,12},{20,16},{24,20},{28,24},{32,28},{36,32}... | collective-permute-start | bytes 24584 | tf_op jit(solution)/shard_map/ppermute | solution.py:35
  61.6 1.9 collective-permute-start.5
  63.6 7.0 %collective-permute-start.2 = (f32[2,4,256]{2,1,0:T(4,128)S(1)}, f32[2,4,256]{2,1,0:T(4,128)S(1)}, u32[]{:S(2)}, u32[]{:S(2)}) collective-permute-start(f32[2,4,256]{2,1,0:T(4,128)S(1)} %get-tuple-element.682), channel_id=1, source_target_pairs={{4,0},{8,4},{12,8},{16,12},{20,16},{24,20},{28,24},{32,28},{36,32}... | collective-permute-start | bytes 24584 | tf_op jit(solution)/shard_map/ppermute | solution.py:35
  70.5 1.9 collective-permute-start.3
  73.1 1.8 copy.215
  74.9 3.9 %collective-permute-done.3 = f32[2,4,256]{2,1,0:T(4,128)S(1)} collective-permute-done((f32[2,4,256]{2,1,0:T(4,128)S(1)}, f32[2,4,256]{2,1,0:T(4,128)S(1)}, u32[]{:S(2)}, u32[]{:S(2)}) %collective-permute-start.3) | collective-permute-done | bytes 8224 | tf_op jit(solution)/shard_map/ppermute | solution.py:35
  78.9 2.1 collective-permute-start.6
  80.9 7.0 %collective-permute-start.7 = (f32[2,2,4,256]{3,2,1,0:T(4,128)S(1)}, f32[2,2,4,256]{3,2,1,0:T(4,128)S(1)}, u32[]{:S(2)}, u32[]{:S(2)}) collective-permute-start(f32[2,2,4,256]{3,2,1,0:T(4,128)S(1)} %pad_maximum_fusion.6), channel_id=1, source_target_pairs={{4,0},{8,4},{12,8},{16,12},{20,16},{24,20},{28,24},{32,28},{36,32}... | collective-permute-start | bytes 49160 | tf_op jit(solution)/shard_map/ppermute | solution.py:25
  90.9 2.9 fusion.76
  95.2 6.8 %collective-permute-start.8 = (f32[512,256]{0,1:T(8,128)S(1)}, f32[512,256]{0,1:T(8,128)}, u32[]{:S(2)}, u32[]{:S(2)}) collective-permute-start(f32[512,256]{0,1:T(8,128)S(1)} %bitcast.454), channel_id=1, source_target_pairs={{4,0},{8,4},{12,8},{16,12},{20,16},{24,20},{28,24},{32,28},{36,32}... | collective-permute-start | bytes 1572872 | tf_op jit(solution)/shard_map/ppermute | solution.py:35
  102.8 1.9 collective-permute-start.9
  104.8 1.6 reshape.294
  106.4 2.5 copy.226
  108.9 1.6 reshape.295
  110.5 2.5 copy.227
  113.0 1.4 reshape.187
  114.4 2.5 collective-permute-done.9
  116.9 1.4 reshape.189
  118.3 2.1 multiply_reduce_fusion
  120.7 8.6 %all-reduce.1 = (f32[512]{0:T(512)S(1)}, f32[512]{0:T(512)S(1)}) all-reduce(f32[512]{0:T(512)S(1)} %bitcast.464, f32[512]{0:T(512)S(1)} %bitcast.465), channel_id=1, replica_groups=mesh['st'=128,'hd'=4] {'hd'}, use_global_device_ids=true, to_apply=%region_9.10 | all-reduce | flops 1024 | bytes 8192 | tf_op jit(solution)/shard_map/psum | solution.py:167
  130.6 10.3 %all-reduce = (f32[512]{0:T(512)S(1)}, f32[512]{0:T(512)S(1)}) all-reduce(f32[512]{0:T(512)S(1)} %fusion.87, f32[512]{0:T(512)S(1)} %fusion.90), channel_id=1, replica_groups=mesh['st'=128,'hd'=4] {'hd'}, use_global_device_ids=true, to_apply=%region_15.16 | all-reduce | flops 1024 | bytes 8192 | tf_op jit(solution)/shard_map/psum | solution.py:178
  141.0 1.9 convert_multiply_fusion.2
  143.6 1.9 collective-permute-start.12
  145.6 7.0 %collective-permute-start.13 = (f32[3,2,4,256]{3,2,1,0:T(4,128)S(1)}, f32[3,2,4,256]{3,2,1,0:T(4,128)S(1)}, u32[]{:S(2)}, u32[]{:S(2)}) collective-permute-start(f32[3,2,4,256]{3,2,1,0:T(4,128)S(1)} %pad_maximum_fusion.5), channel_id=1, source_target_pairs={{4,0},{8,4},{12,8},{16,12},{20,16},{24,20},{28,24},{32,28},{36,32}... | collective-permute-start | bytes 73736 | tf_op jit(solution)/shard_map/ppermute | solution.py:25
  152.5 1.9 collective-permute-start.10
  154.5 7.0 %collective-permute-start.11 = (bf16[512,256]{1,0:T(8,128)(2,1)}, bf16[512,256]{1,0:T(8,128)(2,1)}, u32[]{:S(2)}, u32[]{:S(2)}) collective-permute-start(bf16[512,256]{1,0:T(8,128)(2,1)} %get-tuple-element.643), channel_id=1, source_target_pairs={{4,0},{8,4},{12,8},{16,12},{20,16},{24,20},{28,24},{32,28},{36,32}... | collective-permute-start | bytes 786440 | tf_op jit(solution)/shard_map/ppermute | solution.py:25
  164.2 1.4 collective-permute-done.11
  166.7 1.6 reshape.296
  168.3 3.4 %copy.228 = bf16[6,256,4,64]{1,3,2,0:T(8,128)(2,1)} copy(bf16[6,256,4,64]{3,2,1,0:T(4,128)(2,1)} %reshape.296) | data formatting | bytes 1572864 | tf_op jit(solution)/shard_map/while | solution.py:273
  171.6 1.3 broadcast.141
  173.0 1.4 broadcast.141.clone.1
  174.3 88.1 %while.73 = (s32[]{:T(128)}, bf16[2,256,4,64]{1,3,2,0:T(8,128)(2,1)}, bf16[2,256,4,64]{1,3,2,0:T(8,128)(2,1)}, f32[2,3,256,4,64]{2,4,1,3,0:T(8,128)}, f32[2,3,25...) while((s32[]{:T(128)}, ...), condition=%wide.region_25.26_spmd.clone, body=%wide.region_20.25_spmd.sunk.clone | while | flops 181502480 | bytes 21030028 | solution.py:273
  179.0 1.7 gather_fusion.6
  180.7 1.6 dynamic-slice_bitcast_fusion.15
  184.9 28.9 %while.72 = (s32[]{:T(128)}, bf16[4,256,64]{1,2,0:T(8,128)(2,1)S(1)}, bf16[4,256,64]{1,2,0:T(8,128)(2,1)}, f32[4,3,256,64]{2,3,1,0:T(8,128)}, f32[4,3,256,64]{2,...) while((s32[]{:T(128)}, ...), condition=%wide.region_24.24_spmd, body=%wide.region_21.23_spmd.sunk | while | flops 181501440 | bytes 9187016 | solution.py:251
  188.7 1.3 fusion.161
  213.9 2.7 bitcast_dynamic-update-slice_fusion.21
  223.0 1.7 gather_fusion.6
  224.8 1.6 dynamic-slice_bitcast_fusion.15
  229.0 28.9 %while.72 = (s32[]{:T(128)}, bf16[4,256,64]{1,2,0:T(8,128)(2,1)S(1)}, bf16[4,256,64]{1,2,0:T(8,128)(2,1)}, f32[4,3,256,64]{2,3,1,0:T(8,128)}, f32[4,3,256,64]{2,...) while((s32[]{:T(128)}, ...), condition=%wide.region_24.24_spmd, body=%wide.region_21.23_spmd.sunk | while | flops 181501440 | bytes 9187016 | solution.py:251
  257.9 2.8 bitcast_dynamic-update-slice_fusion.21
  262.5 4.4 %fusion.79 = f32[6,256,4,64]{1,0,3,2:T(8,128)S(1)} fusion(f32[2,3,256,4,64]{2,4,1,3,0:T(8,128)} %get-tuple-element.287, pred[2,3,6]{2,1,0:T(4,128)(4,1)} %copy-done.27), kind=kOutput, calls=%fused_computation.139 | convolution fusion | flops 28311552 | bytes 3145764 | tf_op jit(solution)/shard_map/tsw,tsjhd->wjhd/dot_general | solution.py:277
  266.8 1.7 stack_reshape.6
  268.5 1.6 constant_dynamic-update-slice_fusion.1
  270.4 4.2 %fusion.82 = f32[6,256,4,64]{1,0,3,2:T(8,128)} fusion(f32[2,3,256,4,64]{2,4,1,3,0:T(8,128)S(1)} %copy-done.4, pred[2,3,6]{2,1,0:T(4,128)(4,1)S(1)} %copy-done.28), kind=kOutput, calls=%fused_computation.140 | convolution fusion | flops 28311552 | bytes 3145764 | tf_op jit(solution)/shard_map/tsw,tsjhd->wjhd/dot_general | solution.py:278
  274.5 2.8 stack_reshape.7
  277.3 1.5 constant_dynamic-update-slice_fusion
  280.1 7.1 %collective-permute-start.14 = (bf16[2,512,256]{1,2,0:T(8,128)(2,1)}, bf16[2,512,256]{1,2,0:T(8,128)(2,1)}, u32[]{:S(2)}, u32[]{:S(2)}) collective-permute-start(bf16[2,512,256]{1,2,0:T(8,128)(2,1)} %get-tuple-element.670), channel_id=1, source_target_pairs={{4,0},{8,4},{12,8},{16,12},{20,16},{24,20},{28,24},{32,28},{36,32}... | collective-permute-start | bytes 1572872 | tf_op jit(solution)/shard_map/ppermute | solution.py:35
  287.3 1.9 collective-permute-start.15
  290.0 2.0 copy.256
  292.1 2.2 reshape.297
  295.3 2.2 reshape.298
  297.4 3.9 %collective-permute-done.15 = bf16[2,512,256]{1,2,0:T(8,128)(2,1)} collective-permute-done((bf16[2,512,256]{1,2,0:T(8,128)(2,1)}, bf16[2,512,256]{1,2,0:T(8,128)(2,1)}, u32[]{:S(2)}, u32[]{:S(2)}) %collective-permute-start.15) | collective-permute-done | bytes 524320 | tf_op jit(solution)/shard_map/ppermute | solution.py:35
  301.4 1.4 fusion.86
  (409 shorter events, 124.2 us)
Async XLA Ops:
  0.6 13.0 %copy-start.18 = (bf16[512,256]{1,0:T(8,128)(2,1)S(1)}, bf16[512,256]{1,0:T(8,128)(2,1)}, u32[]{:S(2)}) copy-start(bf16[512,256]{1,0:T(8,128)(2,1)} %param.17) | copy-start | bytes 786436
  1.8 13.9 %collective-permute-start = (bf16[2,512,256]{2,1,0:T(8,128)(2,1)S(1)}, bf16[2,512,256]{2,1,0:T(8,128)(2,1)S(1)}, u32[]{:S(2)}, u32[]{:S(2)}) collective-permute-start(bf16[2,512,256]{2,1,0:T(8,128)(2,1)S(1)} %pad_maximum_fusion.2), channel_id=1, source_target_pairs={{0,4},{4,8},{8,12},{12,16},{16,20},{20,24},{24,28},{28,32},{32,36}... | collective-permute-start | bytes 1572872 | tf_op jit(solution)/shard_map/ppermute | solution.py:23
  3.7 13.6 %collective-permute-start.1 = (bf16[2,512,256]{2,1,0:T(8,128)(2,1)S(1)}, bf16[2,512,256]{2,1,0:T(8,128)(2,1)S(1)}, u32[]{:S(2)}, u32[]{:S(2)}) collective-permute-start(bf16[2,512,256]{2,1,0:T(8,128)(2,1)S(1)} %pad_maximum_fusion.2), channel_id=1, source_target_pairs={{4,0},{8,4},{12,8},{16,12},{20,16},{24,20},{28,24},{32,28},{36,32}... | collective-permute-start | bytes 1572872 | tf_op jit(solution)/shard_map/ppermute | solution.py:25
  11.4 4.1 %copy-start.35 = (s32[2]{0:T(128)S(1)}, s32[2]{0:T(128)}, u32[]{:S(2)}) copy-start(s32[2]{0:T(128)} %param.21) | copy-start | bytes 28
  11.4 6.0 %copy-start.15 = (bf16[512,256]{1,0:T(8,128)(2,1)S(1)}, bf16[512,256]{1,0:T(8,128)(2,1)}, u32[]{:S(2)}) copy-start(bf16[512,256]{1,0:T(8,128)(2,1)} %param.19) | copy-start | bytes 786436
  11.4 6.0 %copy-start.16 = (bf16[512,256]{1,0:T(8,128)(2,1)S(1)}, bf16[512,256]{1,0:T(8,128)(2,1)}, u32[]{:S(2)}) copy-start(bf16[512,256]{1,0:T(8,128)(2,1)} %param.18) | copy-start | bytes 786436
  15.6 75.3 %copy-start.27 = (pred[2,3,6]{2,1,0:T(4,128)(4,1)}, pred[2,3,6]{2,1,0:T(4,128)(4,1)S(1)}, u32[]{:S(2)}) copy-start(pred[2,3,6]{2,1,0:T(4,128)(4,1)S(1)} %fusion.98) | copy-start | bytes 112
  17.5 2.9 copy-start
  36.3 1.2 copy-start.11
  36.3 2.1 copy-start.24
  36.3 2.2 copy-start.29
  38.4 0.8 copy-start.12
  49.7 1.2 copy-start.11
  49.7 2.1 copy-start.24
  49.7 2.2 copy-start.29
  52.7 36.3 %copy-start.13 = (f32[2,256,4,64]{1,3,2,0:T(8,128)S(1)}, f32[2,256,4,64]{1,3,2,0:T(8,128)}, u32[]{:S(2)}) copy-start(f32[2,256,4,64]{1,3,2,0:T(8,128)} %get-tuple-element.281) | copy-start | bytes 1572868
  54.5 20.4 %collective-permute-start.4 = (f32[2,4,256]{2,1,0:T(4,128)S(1)}, f32[2,4,256]{2,1,0:T(4,128)S(1)}, u32[]{:S(2)}, u32[]{:S(2)}) collective-permute-start(f32[2,4,256]{2,1,0:T(4,128)S(1)} %get-tuple-element.684), channel_id=1, source_target_pairs={{4,0},{8,4},{12,8},{16,12},{20,16},{24,20},{28,24},{32,28},{36,32}... | collective-permute-start | bytes 24584 | tf_op jit(solution)/shard_map/ppermute | solution.py:35
  61.6 13.3 %collective-permute-start.5 = (f32[2,4,256]{2,1,0:T(4,128)S(1)}, f32[2,4,256]{2,1,0:T(4,128)S(1)}, u32[]{:S(2)}, u32[]{:S(2)}) collective-permute-start(f32[2,4,256]{2,1,0:T(4,128)S(1)} %get-tuple-element.685), channel_id=1, source_target_pairs={{0,4},{4,8},{8,12},{12,16},{16,20},{20,24},{24,28},{28,32},{32,36}... | collective-permute-start | bytes 24584 | tf_op jit(solution)/shard_map/ppermute | solution.py:35
  63.6 11.3 %collective-permute-start.2 = (f32[2,4,256]{2,1,0:T(4,128)S(1)}, f32[2,4,256]{2,1,0:T(4,128)S(1)}, u32[]{:S(2)}, u32[]{:S(2)}) collective-permute-start(f32[2,4,256]{2,1,0:T(4,128)S(1)} %get-tuple-element.682), channel_id=1, source_target_pairs={{4,0},{8,4},{12,8},{16,12},{20,16},{24,20},{28,24},{32,28},{36,32}... | collective-permute-start | bytes 24584 | tf_op jit(solution)/shard_map/ppermute | solution.py:35
  70.5 8.3 %collective-permute-start.3 = (f32[2,4,256]{2,1,0:T(4,128)S(1)}, f32[2,4,256]{2,1,0:T(4,128)S(1)}, u32[]{:S(2)}, u32[]{:S(2)}) collective-permute-start(f32[2,4,256]{2,1,0:T(4,128)S(1)} %get-tuple-element.683), channel_id=1, source_target_pairs={{0,4},{4,8},{8,12},{12,16},{16,20},{20,24},{24,28},{28,32},{32,36}... | collective-permute-start | bytes 24584 | tf_op jit(solution)/shard_map/ppermute | solution.py:35
  74.9 15.8 %copy-start.26 = (f32[2,3,4,256]{3,2,1,0:T(4,128)S(1)}, f32[2,3,4,256]{3,2,1,0:T(4,128)}, u32[]{:S(2)}) copy-start(f32[2,3,4,256]{3,2,1,0:T(4,128)} %get-tuple-element.283) | copy-start | bytes 73732
  78.8 11.9 %copy-start.6 = (f32[2,3,256,4,64]{2,4,1,3,0:T(8,128)S(1)}, f32[2,3,256,4,64]{2,4,1,3,0:T(8,128)}, u32[]{:S(2)}) copy-start(f32[2,3,256,4,64]{2,4,1,3,0:T(8,128)} %get-tuple-element.282) | copy-start | bytes 4718596
  78.9 10.6 %collective-permute-start.6 = (f32[2,2,4,256]{3,2,1,0:T(4,128)S(1)}, f32[2,2,4,256]{3,2,1,0:T(4,128)S(1)}, u32[]{:S(2)}, u32[]{:S(2)}) collective-permute-start(f32[2,2,4,256]{3,2,1,0:T(4,128)S(1)} %pad_maximum_fusion.6), channel_id=1, source_target_pairs={{0,4},{4,8},{8,12},{12,16},{16,20},{20,24},{24,28},{28,32},{32,36}... | collective-permute-start | bytes 49160 | tf_op jit(solution)/shard_map/ppermute | solution.py:23
  80.9 8.6 %collective-permute-start.7 = (f32[2,2,4,256]{3,2,1,0:T(4,128)S(1)}, f32[2,2,4,256]{3,2,1,0:T(4,128)S(1)}, u32[]{:S(2)}, u32[]{:S(2)}) collective-permute-start(f32[2,2,4,256]{3,2,1,0:T(4,128)S(1)} %pad_maximum_fusion.6), channel_id=1, source_target_pairs={{4,0},{8,4},{12,8},{16,12},{20,16},{24,20},{28,24},{32,28},{36,32}... | collective-permute-start | bytes 49160 | tf_op jit(solution)/shard_map/ppermute | solution.py:25
  93.9 1.3 copy-start.5
  94.3 10.4 %copy-start.1 = (bf16[2,1536,256]{2,1,0:T(8,128)(2,1)S(1)}, bf16[2,1536,256]{2,1,0:T(8,128)(2,1)}, u32[]{:S(2)}) copy-start(bf16[2,1536,256]{2,1,0:T(8,128)(2,1)} %copy-done) | copy-start | bytes 4718596
  95.2 17.8 %collective-permute-start.8 = (f32[512,256]{0,1:T(8,128)S(1)}, f32[512,256]{0,1:T(8,128)}, u32[]{:S(2)}, u32[]{:S(2)}) collective-permute-start(f32[512,256]{0,1:T(8,128)S(1)} %bitcast.454), channel_id=1, source_target_pairs={{4,0},{8,4},{12,8},{16,12},{20,16},{24,20},{28,24},{32,28},{36,32}... | collective-permute-start | bytes 1572872 | tf_op jit(solution)/shard_map/ppermute | solution.py:35
  102.8 14.1 %collective-permute-start.9 = (f32[512,256]{0,1:T(8,128)}, f32[512,256]{0,1:T(8,128)}, u32[]{:S(2)}, u32[]{:S(2)}) collective-permute-start(f32[512,256]{0,1:T(8,128)} %bitcast.141), channel_id=1, source_target_pairs={{0,4},{4,8},{8,12},{12,16},{16,20},{20,24},{24,28},{28,32},{32,36}... | collective-permute-start | bytes 1572872 | tf_op jit(solution)/shard_map/ppermute | solution.py:35
  120.5 10.1 %copy-start.10 = (bf16[512,256]{0,1:T(8,128)(2,1)S(1)}, bf16[512,256]{0,1:T(8,128)(2,1)}, u32[]{:S(2)}) copy-start(bf16[512,256]{0,1:T(8,128)(2,1)} %copy.215) | copy-start | bytes 786436
  143.6 20.5 %collective-permute-start.12 = (f32[3,2,4,256]{3,2,1,0:T(4,128)S(1)}, f32[3,2,4,256]{3,2,1,0:T(4,128)S(1)}, u32[]{:S(2)}, u32[]{:S(2)}) collective-permute-start(f32[3,2,4,256]{3,2,1,0:T(4,128)S(1)} %pad_maximum_fusion.5), channel_id=1, source_target_pairs={{0,4},{4,8},{8,12},{12,16},{16,20},{20,24},{24,28},{28,32},{32,36}... | collective-permute-start | bytes 73736 | tf_op jit(solution)/shard_map/ppermute | solution.py:23
  145.6 18.6 %collective-permute-start.13 = (f32[3,2,4,256]{3,2,1,0:T(4,128)S(1)}, f32[3,2,4,256]{3,2,1,0:T(4,128)S(1)}, u32[]{:S(2)}, u32[]{:S(2)}) collective-permute-start(f32[3,2,4,256]{3,2,1,0:T(4,128)S(1)} %pad_maximum_fusion.5), channel_id=1, source_target_pairs={{4,0},{8,4},{12,8},{16,12},{20,16},{24,20},{28,24},{32,28},{36,32}... | collective-permute-start | bytes 73736 | tf_op jit(solution)/shard_map/ppermute | solution.py:25
  152.5 11.7 %collective-permute-start.10 = (bf16[512,256]{1,0:T(8,128)(2,1)}, bf16[512,256]{1,0:T(8,128)(2,1)}, u32[]{:S(2)}, u32[]{:S(2)}) collective-permute-start(bf16[512,256]{1,0:T(8,128)(2,1)} %get-tuple-element.643), channel_id=1, source_target_pairs={{0,4},{4,8},{8,12},{12,16},{16,20},{20,24},{24,28},{28,32},{32,36}... | collective-permute-start | bytes 786440 | tf_op jit(solution)/shard_map/ppermute | solution.py:23
  154.5 11.2 %collective-permute-start.11 = (bf16[512,256]{1,0:T(8,128)(2,1)}, bf16[512,256]{1,0:T(8,128)(2,1)}, u32[]{:S(2)}, u32[]{:S(2)}) collective-permute-start(bf16[512,256]{1,0:T(8,128)(2,1)} %get-tuple-element.643), channel_id=1, source_target_pairs={{4,0},{8,4},{12,8},{16,12},{20,16},{24,20},{28,24},{32,28},{36,32}... | collective-permute-start | bytes 786440 | tf_op jit(solution)/shard_map/ppermute | solution.py:25
  162.3 3.3 %copy-start.17 = (bf16[512,256]{1,0:T(8,128)(2,1)S(1)}, bf16[512,256]{1,0:T(8,128)(2,1)}, u32[]{:S(2)}) copy-start(bf16[512,256]{1,0:T(8,128)(2,1)} %get-tuple-element.643) | copy-start | bytes 786436
  171.6 2.7 copy-start.2
  171.6 2.7 copy-start.3
  174.3 4.1 %copy-start.8 = (f32[3,6,4,256]{3,2,1,0:T(4,128)}, f32[3,6,4,256]{3,2,1,0:T(4,128)S(1)}, u32[]{:S(2)}) copy-start(f32[3,6,4,256]{3,2,1,0:T(4,128)S(1)} %get-tuple-element.1364) | copy-start | bytes 221188 | tf_op jit(solution)/shard_map/while
  174.3 4.6 %copy-start.33 = (pred[2,3]{1,0:T(4,128)(4,1)}, pred[2,3]{1,0:T(4,128)(4,1)S(1)}, u32[]{:S(2)}) copy-start(pred[2,3]{1,0:T(4,128)(4,1)S(1)} %get-tuple-element.1365) | copy-start | bytes 22 | tf_op jit(solution)/shard_map/while
  184.9 0.9 copy-start.7
  192.2 0.9 copy-start.7
  199.4 0.9 copy-start.7
  206.6 0.9 copy-start.7
  213.9 2.8 copy-start.19
  213.9 2.8 copy-start.21
  213.9 4.5 %copy-start.9 = (f32[3,6,4,256]{3,2,1,0:T(4,128)S(1)}, f32[3,6,4,256]{3,2,1,0:T(4,128)}, u32[]{:S(2)}) copy-start(f32[3,6,4,256]{3,2,1,0:T(4,128)} %copy-done.8) | copy-start | bytes 221188 | tf_op jit(solution)/shard_map/while
  213.9 4.5 %copy-start.32 = (s32[2,3]{1,0:T(2,128)S(1)}, s32[2,3]{1,0:T(2,128)}, u32[]{:S(2)}) copy-start(s32[2,3]{1,0:T(2,128)} %copy-done.31) | copy-start | bytes 76 | tf_op jit(solution)/shard_map/while
  213.9 4.5 %copy-start.34 = (pred[2,3]{1,0:T(4,128)(4,1)S(1)}, pred[2,3]{1,0:T(4,128)(4,1)}, u32[]{:S(2)}) copy-start(pred[2,3]{1,0:T(4,128)(4,1)} %copy-done.33) | copy-start | bytes 22 | tf_op jit(solution)/shard_map/while
  218.4 4.1 %copy-start.8 = (f32[3,6,4,256]{3,2,1,0:T(4,128)}, f32[3,6,4,256]{3,2,1,0:T(4,128)S(1)}, u32[]{:S(2)}) copy-start(f32[3,6,4,256]{3,2,1,0:T(4,128)S(1)} %get-tuple-element.1364) | copy-start | bytes 221188 | tf_op jit(solution)/shard_map/while
  218.4 4.6 %copy-start.33 = (pred[2,3]{1,0:T(4,128)(4,1)}, pred[2,3]{1,0:T(4,128)(4,1)S(1)}, u32[]{:S(2)}) copy-start(pred[2,3]{1,0:T(4,128)(4,1)S(1)} %get-tuple-element.1365) | copy-start | bytes 22 | tf_op jit(solution)/shard_map/while
  229.0 0.9 copy-start.7
  236.2 0.9 copy-start.7
  243.4 0.9 copy-start.7
  250.7 0.9 copy-start.7
  257.9 2.8 copy-start.19
  257.9 2.8 copy-start.21
  257.9 4.5 %copy-start.9 = (f32[3,6,4,256]{3,2,1,0:T(4,128)S(1)}, f32[3,6,4,256]{3,2,1,0:T(4,128)}, u32[]{:S(2)}) copy-start(f32[3,6,4,256]{3,2,1,0:T(4,128)} %copy-done.8) | copy-start | bytes 221188 | tf_op jit(solution)/shard_map/while
  257.9 4.5 %copy-start.32 = (s32[2,3]{1,0:T(2,128)S(1)}, s32[2,3]{1,0:T(2,128)}, u32[]{:S(2)}) copy-start(s32[2,3]{1,0:T(2,128)} %copy-done.31) | copy-start | bytes 76 | tf_op jit(solution)/shard_map/while
  257.9 4.5 %copy-start.34 = (pred[2,3]{1,0:T(4,128)(4,1)S(1)}, pred[2,3]{1,0:T(4,128)(4,1)}, u32[]{:S(2)}) copy-start(pred[2,3]{1,0:T(4,128)(4,1)} %copy-done.33) | copy-start | bytes 22 | tf_op jit(solution)/shard_map/while
  268.5 1.9 copy-start.4
  268.5 1.9 copy-start.28
  279.0 10.2 %copy-start.14 = (bf16[512,256]{0,1:T(8,128)(2,1)S(1)}, bf16[512,256]{0,1:T(8,128)(2,1)}, u32[]{:S(2)}) copy-start(bf16[512,256]{0,1:T(8,128)(2,1)} %get-tuple-element.675) | copy-start | bytes 786436
  280.1 17.3 %collective-permute-start.14 = (bf16[2,512,256]{1,2,0:T(8,128)(2,1)}, bf16[2,512,256]{1,2,0:T(8,128)(2,1)}, u32[]{:S(2)}, u32[]{:S(2)}) collective-permute-start(bf16[2,512,256]{1,2,0:T(8,128)(2,1)} %get-tuple-element.670), channel_id=1, source_target_pairs={{4,0},{8,4},{12,8},{16,12},{20,16},{24,20},{28,24},{32,28},{36,32}... | collective-permute-start | bytes 1572872 | tf_op jit(solution)/shard_map/ppermute | solution.py:35
  287.3 14.1 %collective-permute-start.15 = (bf16[2,512,256]{1,2,0:T(8,128)(2,1)}, bf16[2,512,256]{1,2,0:T(8,128)(2,1)}, u32[]{:S(2)}, u32[]{:S(2)}) collective-permute-start(bf16[2,512,256]{1,2,0:T(8,128)(2,1)} %get-tuple-element.671), channel_id=1, source_target_pairs={{0,4},{4,8},{8,12},{12,16},{16,20},{20,24},{24,28},{28,32},{32,36}... | collective-permute-start | bytes 1572872 | tf_op jit(solution)/shard_map/ppermute | solution.py:35
  290.0 4.2 %copy-start.23 = (bf16[2,256,4,64]{1,3,2,0:T(8,128)(2,1)S(1)}, bf16[2,256,4,64]{1,3,2,0:T(8,128)(2,1)}, u32[]{:S(2)}) copy-start(bf16[2,256,4,64]{1,3,2,0:T(8,128)(2,1)} %get-tuple-element.286) | copy-start | bytes 786436
  (11 other events, 8.0 us)
where the time goes:
time: 308 us; the launch traced here: 305 us
  local copies, waits for them, and re-layouts  112 us (36%)
  starting transfers between devices  71.3 us (23%)
  matrix products  66 us (21%)
  other arithmetic  20.5 us (7%)
  blocking collectives  18.9 us (6%)
  waiting for transfers between devices  13.5 us (4%)
    ppermute x8, starting transfers between devices, shifted(): lax.ppermute(value, axis, [(source, source + steps) for source in range(f...  35.7 us
    ppermute x4, starting transfers between devices, extended(): lax.ppermute(head, axis, [((i + 1) % count, i) for i in range(ends)])  27.8 us
    unnamed x53, local copies, waits for them, and re-layouts  15.5 us
    dynamic_slice x48, local copies, waits for them, and re-layouts, backward_block(): lax.map(backward_head, (heads_first(queries), heads_first(values), heads_...  11.5 us
    ppermute x8, waiting for transfers between devices, shifted(): lax.ppermute(value, axis, [(source, source + steps) for source in range(f...  10.4 us
    psum x1, blocking collectives, on_device(): lax.psum((jnp.sum(event_cot * event_normed, axis=1), jnp.sum(frame_cot *...  10.3 us
    dot_general x8, matrix products, backward_head(): jnp.einsum('id,sjd->isj', head_v, head_fg, preferred_element_type=jnp.flo...  10.2 us
    dynamic_update_slice x10, local copies, waits for them, and re-layouts, on_device(): lax.map(forward_block, (query_blocks, value_blocks, window_slot, live))  9.45 us
  transfers between devices with their start and end apart: 16, of which 5 were waited for; matrix products, arithmetic and copies ran while one was open for 10% of the time, Pallas kernels for 0%

commit v1 on v0

v1 whole, which is shorter than its diff:
```python
import jax
import jax.numpy as jnp
from jax import lax
from jax.experimental import pallas as pl
from jax.experimental.pallas import tpu as pltpu
from jax.sharding import PartitionSpec as P

DH = 64
BLOCK = 256
SLOTS = 3
HEADS = 4
FEATS = HEADS * DH
ROWS = 2 * BLOCK
PAIR = 2 * DH
EPS = 1e-06
NEG = -1e30
LOG2E = 1.4426950408889634
SCALE = DH**-0.5

KEYS, FVALS, QUERIES, EVALS, CODES = 0, ROWS, 2 * ROWS, 3 * ROWS, 4 * ROWS
MSG1 = 4 * ROWS + 16
STATS = 2 * ROWS
MSG2 = 2 * ROWS + 4 * 32

F32 = jnp.float32
BF16 = jnp.bfloat16
VMEM_LIMIT = 48 * 1024 * 1024


def dot(a, b):
    return jnp.dot(a, b, preferred_element_type=F32)


def params(**more):
    return pltpu.CompilerParams(vmem_limit_bytes=VMEM_LIMIT, **more)


def cost(flops):
    return pl.CostEstimate(flops=int(flops), bytes_accessed=1 << 20, transcendentals=0)


def neighbours(run):
    odd = lax.rem(run, 2)
    return run + 1 - 2 * odd, run - 1 + 2 * odd


def code_for(partner, live, run):
    code = jnp.int32(0)
    for a in range(2):
        for s in range(SLOTS):
            block = partner[a, s] - 2 * run
            hit = (s < live[a]) & (block >= 0) & (block < 2)
            code += jnp.where(hit, jnp.left_shift(1, 2 * a + jnp.clip(block, 0, 1)), 0)
    return code


def pair_list(todo, partner, live, sources):
    run = lax.axis_index("st")
    count = jnp.int32(0)

    def add(count, hit, self_block, place, block):
        todo[count] = self_block * 8 + place * 2 + block
        return count + hit.astype(jnp.int32)

    for place, (target, code) in enumerate(sources):
        for a in range(2):
            for s in range(SLOTS):
                block = partner[a, s] - 2 * target
                hit = (s < live[a]) & (block >= 0) & (block < 2)
                count = add(count, hit, a, place, block)
                if code is None:
                    count = add(count, hit, 2 + block, place, a)
            if code is not None:
                for f in range(2):
                    hit = jnp.bitwise_and(jnp.right_shift(code, 2 * a + f), 1) == 1
                    count = add(count, hit, 2 + f, place, a)
    return count


def read_code(rows, half):
    part = rows[:, half * PAIR : (half + 1) * PAIR].astype(F32)
    return jnp.max(part).astype(jnp.int32)


def masked(features_first, head):
    low = (head // 2) * PAIR
    tile = features_first[low : low + PAIR, :]
    row = lax.broadcasted_iota(jnp.int32, tile.shape, 0)
    return jnp.where(row // DH == head % 2, tile, jnp.zeros_like(tile))


def pack_kernel(partner, live, queries, event_values, keys, frame_values, msg):
    run = lax.axis_index("st")
    inner, outer = neighbours(run)
    msg[KEYS : KEYS + ROWS, :] = keys[...]
    msg[FVALS : FVALS + ROWS, :] = frame_values[...]
    msg[QUERIES : QUERIES + ROWS, :] = queries[...]
    msg[EVALS : EVALS + ROWS, :] = event_values[...]
    for half, target in enumerate((inner, outer)):
        code = code_for(partner, live, target).astype(F32)
        msg[CODES:MSG1, half * PAIR : (half + 1) * PAIR] = jnp.full((16, PAIR), code, F32).astype(BF16)


def attend(buf, vals_t, self_a, soft, acc, todo, count):
    def pair(n, _):
        entry = todo[n]
        me = lax.div(entry, 8)
        side = lax.div(me, 2)
        place = lax.div(lax.rem(entry, 8), 2)
        block = lax.rem(entry, 2)
        row = pl.multiple_of(side * (2 * ROWS) + block * BLOCK, BLOCK)
        at = place * 4 + side * 2 + block
        for h in range(HEADS):
            low = (h // 2) * PAIR
            other = buf[place, pl.ds(row, BLOCK), low : low + PAIR]
            scores = dot(other, self_a[me, h]) * LOG2E
            old_top = soft[me, h : h + 1, :]
            top = jnp.maximum(old_top, jnp.max(scores, axis=0, keepdims=True))
            weights = jnp.exp2(scores - top)
            decay = jnp.exp2(old_top - top)
            soft[me, h : h + 1, :] = top
            soft[me, HEADS + h : HEADS + h + 1, :] = soft[
                me, HEADS + h : HEADS + h + 1, :
            ] * decay + jnp.sum(weights, axis=0, keepdims=True)
            got = dot(vals_t[at, h * DH : (h + 1) * DH, :], weights.astype(BF16))
            acc[me, h * DH : (h + 1) * DH, :] = acc[me, h * DH : (h + 1) * DH, :] * decay + got
        return 0

    lax.fori_loop(0, count, pair, 0)


def other_values(buf, vals_t, place):
    for side, base in ((0, FVALS), (1, EVALS)):
        for block in range(2):
            low = base + block * BLOCK
            vals_t[place * 4 + side * 2 + block] = buf[place, low : low + BLOCK, :].T


def near_forward(
    partner, live, own, near, event_cot, frame_cot, self_a, self_v, cot_t, soft, acc, buf, vals_t, todo, sems
):
    copies = [pltpu.make_async_copy(src, buf.at[i], sems.at[i]) for i, src in enumerate((own, near))]
    for c in copies:
        c.start()
    for c in copies:
        c.wait()
    for side, (base_a, base_v) in enumerate(((QUERIES, EVALS), (KEYS, FVALS))):
        for block in range(2):
            me = side * 2 + block
            low = block * BLOCK
            a_t = buf[0, base_a + low : base_a + low + BLOCK, :].T * BF16(SCALE)
            v_t = buf[0, base_v + low : base_v + low + BLOCK, :].T
            for h in range(HEADS):
                self_a[me, h] = masked(a_t, h)
                self_v[me, h] = masked(v_t, h)
            cot = (event_cot, frame_cot)[side]
            cot_t[me] = cot[low : low + BLOCK, :].T
            soft[me, 0:HEADS, :] = jnp.full((HEADS, BLOCK), NEG, F32)
            soft[me, HEADS : 2 * HEADS, :] = jnp.zeros((HEADS, BLOCK), F32)
            acc[me] = jnp.zeros((FEATS, BLOCK), F32)
    other_values(buf, vals_t, 0)
    other_values(buf, vals_t, 1)
    run = lax.axis_index("st")
    inner, _ = neighbours(run)
    code = read_code(buf[1, CODES:MSG1, :], 0)
    count = pair_list(todo, partner, live, ((run, None), (inner, code)))
    attend(buf, vals_t, self_a, soft, acc, todo, count)


def far_forward(
    partner, live, far, self_a, cot_t, soft_in, acc_in, att, lse, sums, buf, soft, acc, vals_t, todo, sems
):
    copies = [
        pltpu.make_async_copy(far, buf.at[0], sems.at[0]),
        pltpu.make_async_copy(soft_in, soft, sems.at[1]),
        pltpu.make_async_copy(acc_in, acc, sems.at[2]),
    ]
    for c in copies:
        c.start()
    for c in copies:
        c.wait()
    other_values(buf, vals_t, 0)
    run = lax.axis_index("st")
    _, outer = neighbours(run)
    code = read_code(buf[0, CODES:MSG1, :], 1)
    count = pair_list(todo, partner, live, ((outer, code),))
    attend(buf, vals_t, self_a, soft, acc, todo, count)
    for me in range(4):
        square = jnp.zeros((1, BLOCK), F32)
        slope = jnp.zeros((1, BLOCK), F32)
        for h in range(HEADS):
            total = soft[me, HEADS + h : HEADS + h + 1, :]
            lse[me, h : h + 1, :] = soft[me, h : h + 1, :] + jnp.log2(total)
            part = acc[me, h * DH : (h + 1) * DH, :] * (1.0 / total)
            att[me, h * DH : (h + 1) * DH, :] = part
            square += jnp.sum(part * part, axis=0, keepdims=True)
            cot = cot_t[me, h * DH : (h + 1) * DH, :].astype(F32)
            slope += jnp.sum(part * cot, axis=0, keepdims=True)
        lse[me, HEADS : 2 * HEADS, :] = jnp.zeros((HEADS, BLOCK), F32)
        sums[2 * me : 2 * me + 1, :] = square
        sums[2 * me + 1 : 2 * me + 2, :] = slope


def split(value):
    high = value.astype(BF16).astype(F32)
    rest = value - high
    middle = rest.astype(BF16).astype(F32)
    return high, middle, rest - middle


def grad_kernel(width, att, cot_t, lse, sums, grad_t, normed_t, stats, msg):
    for me in range(4):
        rms = lax.rsqrt(sums[2 * me : 2 * me + 1, :] / width + EPS)
        slope = rms * sums[2 * me + 1 : 2 * me + 2, :] / width
        values = att[me]
        normed = values * rms
        grad = (rms * (cot_t[me].astype(F32) - normed * slope)).astype(BF16)
        grad_t[me] = grad
        normed_t[me] = normed.astype(BF16)
        low = ROWS * (1 - me // 2) + (me % 2) * BLOCK
        msg[low : low + BLOCK, :] = grad.T
        product = grad.astype(F32) * values
        deltas = [
            jnp.sum(product[h * DH : (h + 1) * DH, :], axis=0, keepdims=True) for h in range(HEADS)
        ]
        mine = jnp.concatenate([lse[me, 0:HEADS, :]] + deltas, axis=0)
        stats[me] = mine
        rows = jnp.concatenate(split(mine) + (jnp.zeros_like(mine),), axis=0)
        at = STATS + 32 * (2 * (1 - me // 2) + me % 2)
        msg[at : at + 32, :] = rows.astype(BF16)


def other_grads(buf1, buf2, a_t, g_t, columns, place):
    for side, base in ((0, KEYS), (1, QUERIES)):
        for block in range(2):
            at = place * 4 + side * 2 + block
            low = block * BLOCK
            a_t[at] = buf1[place, base + low : base + low + BLOCK, :].T
            low += side * ROWS
            g_t[at] = buf2[place, low : low + BLOCK, :].T
            low = STATS + 32 * (side * 2 + block)
            rows = buf2[place, low : low + 32, :].astype(F32)
            whole = rows[0:8, :] + rows[8:16, :] + rows[16:24, :]
            padded = jnp.concatenate([whole, jnp.zeros((PAIR - 8, BLOCK), F32)], axis=0)
            columns[at] = padded.T


def back(buf1, buf2, a_t, g_t, columns, self_a, self_v, self_g, stats, grad_a, grad_v, todo, count):
    def pair(n, _):
        entry = todo[n]
        me = lax.div(entry, 8)
        side = lax.div(me, 2)
        place = lax.div(lax.rem(entry, 8), 2)
        block = lax.rem(entry, 2)
        row_a = pl.multiple_of(side * (2 * ROWS) + block * BLOCK, BLOCK)
        row_v = pl.multiple_of(side * (2 * ROWS) + ROWS + block * BLOCK, BLOCK)
        row_g = pl.multiple_of(side * ROWS + block * BLOCK, BLOCK)
        at = place * 4 + side * 2 + block
        for h in range(HEADS):
            low = (h // 2) * PAIR
            lanes = slice(low, low + PAIR)
            head = slice(h * DH, (h + 1) * DH)
            scores = dot(buf1[place, pl.ds(row_a, BLOCK), lanes], self_a[me, h]) * LOG2E
            self_p = jnp.exp2(scores - stats[me, h : h + 1, :])
            other_p = jnp.exp2(scores - columns[at, :, h : h + 1])
            self_change = dot(buf1[place, pl.ds(row_v, BLOCK), lanes], self_g[me, h])
            other_change = dot(buf2[place, pl.ds(row_g, BLOCK), lanes], self_v[me, h])
            slope = self_p * (self_change - stats[me, HEADS + h : HEADS + h + 1, :]) + other_p * (
                other_change - columns[at, :, HEADS + h : HEADS + h + 1]
            )
            grad_a[me, head, :] += dot(a_t[at, head, :], slope.astype(BF16))
            grad_v[me, head, :] += dot(g_t[at, head, :], other_p.astype(BF16))
        return 0

    lax.fori_loop(0, count, pair, 0)


def near_backward(
    partner,
    live,
    own1,
    near1,
    own2,
    near2,
    self_a,
    self_v,
    grad_t,
    normed_t,
    stats,
    event_out,
    frame_out,
    self_g,
    grad_a,
    grad_v,
    buf1,
    buf2,
    a_t,
    g_t,
    columns,
    todo,
    sems,
):
    copies = [
        pltpu.make_async_copy(own1, buf1.at[0], sems.at[0]),
        pltpu.make_async_copy(near1, buf1.at[1], sems.at[1]),
        pltpu.make_async_copy(own2, buf2.at[0], sems.at[2]),
        pltpu.make_async_copy(near2, buf2.at[1], sems.at[3]),
    ]
    for c in copies:
        c.start()
    for me in range(4):
        out = (event_out, frame_out)[me // 2]
        low = (me % 2) * BLOCK
        out[low : low + BLOCK, :] = normed_t[me].T
        for h in range(HEADS):
            self_g[me, h] = masked(grad_t[me], h)
        grad_a[me] = jnp.zeros((FEATS, BLOCK), F32)
        grad_v[me] = jnp.zeros((FEATS, BLOCK), F32)
    for c in copies:
        c.wait()
    other_grads(buf1, buf2, a_t, g_t, columns, 0)
    other_grads(buf1, buf2, a_t, g_t, columns, 1)
    run = lax.axis_index("st")
    inner, _ = neighbours(run)
    code = read_code(buf1[1, CODES:MSG1, :], 0)
    count = pair_list(todo, partner, live, ((run, None), (inner, code)))
    back(buf1, buf2, a_t, g_t, columns, self_a, self_v, self_g, stats, grad_a, grad_v, todo, count)


def far_backward(
    partner,
    live,
    far1,
    far2,
    self_a,
    self_v,
    self_g,
    stats,
    grad_a_in,
    grad_v_in,
    grad_queries,
    grad_event_values,
    grad_keys,
    grad_frame_values,
    buf1,
    buf2,
    grad_a,
    grad_v,
    a_t,
    g_t,
    columns,
    todo,
    sems,
):
    copies = [
        pltpu.make_async_copy(far1, buf1.at[0], sems.at[0]),
        pltpu.make_async_copy(far2, buf2.at[0], sems.at[1]),
        pltpu.make_async_copy(grad_a_in, grad_a, sems.at[2]),
        pltpu.make_async_copy(grad_v_in, grad_v, sems.at[3]),
    ]
    for c in copies:
        c.start()
    for c in copies:
        c.wait()
    other_grads(buf1, buf2, a_t, g_t, columns, 0)
    run = lax.axis_index("st")
    _, outer = neighbours(run)
    code = read_code(buf1[0, CODES:MSG1, :], 1)
    count = pair_list(todo, partner, live, ((outer, code),))
    back(buf1, buf2, a_t, g_t, columns, self_a, self_v, self_g, stats, grad_a, grad_v, todo, count)
    for me in range(4):
        low = (me % 2) * BLOCK
        out_a, out_v = ((grad_queries, grad_event_values), (grad_keys, grad_frame_values))[me // 2]
        out_a[low : low + BLOCK, :] = (grad_a[me] * SCALE).astype(BF16).T
        out_v[low : low + BLOCK, :] = grad_v[me].astype(BF16).T


def shape(*dims, dtype=F32):
    return jax.ShapeDtypeStruct(dims, dtype)


def specs(*kinds):
    space = {"s": pltpu.SMEM, "v": pltpu.VMEM, "h": pl.ANY}
    return [pl.BlockSpec(memory_space=space[k]) for k in "".join(kinds)]


def on_device(
    event_queries,
    event_values,
    frame_keys,
    frame_values,
    partner,
    live_count,
    event_cotangent,
    frame_cotangent,
):
    width = FEATS * lax.axis_size("hd")
    runs = lax.axis_size("st")
    inner_pairs = [(i, i ^ 1) for i in range(runs)]
    outer_pairs = [(i, i + 1) for i in range(1, runs - 1, 2)] + [(i + 1, i) for i in range(1, runs - 1, 2)]
    tile = (4, FEATS, BLOCK)
    wide = (4, HEADS, PAIR, BLOCK)
    todo = pltpu.SMEM((40,), jnp.int32)

    msg = pl.pallas_call(
        pack_kernel,
        out_shape=shape(MSG1, FEATS, dtype=BF16),
        in_specs=specs("ssvvvv"),
        out_specs=specs("v")[0],
        compiler_params=params(),
    )(partner, live_count, event_queries, event_values, frame_keys, frame_values)
    far = lax.ppermute(msg, "st", outer_pairs)
    near = lax.ppermute(msg, "st", inner_pairs)

    self_a, self_v, cot_t, soft, acc = pl.pallas_call(
        near_forward,
        out_shape=(
            shape(*wide, dtype=BF16),
            shape(*wide, dtype=BF16),
            shape(*tile, dtype=BF16),
            shape(4, 2 * HEADS, BLOCK),
            shape(*tile),
        ),
        in_specs=specs("sshhvv"),
        out_specs=tuple(specs("vvvvv")),
        scratch_shapes=[
            pltpu.VMEM((2, MSG1, FEATS), BF16),
            pltpu.VMEM((8, FEATS, BLOCK), BF16),
            todo,
            pltpu.SemaphoreType.DMA((2,)),
        ],
        compiler_params=params(),
        cost_estimate=cost(5e9),
    )(partner, live_count, msg, near, event_cotangent, frame_cotangent)

    att, lse, sums = pl.pallas_call(
        far_forward,
        out_shape=(shape(*tile), shape(4, 2 * HEADS, BLOCK), shape(8, BLOCK)),
        in_specs=specs("sshvvhh"),
        out_specs=tuple(specs("vvv")),
        scratch_shapes=[
            pltpu.VMEM((1, MSG1, FEATS), BF16),
            pltpu.VMEM((4, 2 * HEADS, BLOCK), F32),
            pltpu.VMEM(tile, F32),
            pltpu.VMEM((4, FEATS, BLOCK), BF16),
            todo,
            pltpu.SemaphoreType.DMA((3,)),
        ],
        compiler_params=params(),
        cost_estimate=cost(3e9),
    )(partner, live_count, far, self_a, cot_t, soft, acc)
    sums = lax.psum(sums, "hd")

    grad_t, normed_t, stats, msg2 = pl.pallas_call(
        lambda *refs: grad_kernel(width, *refs),
        out_shape=(
            shape(*tile, dtype=BF16),
            shape(*tile, dtype=BF16),
            shape(4, 2 * HEADS, BLOCK),
            shape(MSG2, FEATS, dtype=BF16),
        ),
        in_specs=specs("vvvv"),
        out_specs=tuple(specs("vvvv")),
        compiler_params=params(),
        cost_estimate=cost(1e9),
    )(att, cot_t, lse, sums)
    far2 = lax.ppermute(msg2, "st", outer_pairs)
    near2 = lax.ppermute(msg2, "st", inner_pairs)

    event_out, frame_out, self_g, grad_a, grad_v = pl.pallas_call(
        near_backward,
        out_shape=(
            shape(ROWS, FEATS, dtype=BF16),
            shape(ROWS, FEATS, dtype=BF16),
            shape(*wide, dtype=BF16),
            shape(*tile),
            shape(*tile),
        ),
        in_specs=specs("sshhhhvvvvv"),
        out_specs=tuple(specs("vvvvv")),
        scratch_shapes=[
            pltpu.VMEM((2, MSG1, FEATS), BF16),
            pltpu.VMEM((2, MSG2, FEATS), BF16),
            pltpu.VMEM((8, FEATS, BLOCK), BF16),
            pltpu.VMEM((8, FEATS, BLOCK), BF16),
            pltpu.VMEM((8, BLOCK, PAIR), F32),
            todo,
            pltpu.SemaphoreType.DMA((4,)),
        ],
        compiler_params=params(),
        cost_estimate=cost(8e9),
    )(partner, live_count, msg, near, msg2, near2, self_a, self_v, grad_t, normed_t, stats)

    grads = pl.pallas_call(
        far_backward,
        out_shape=tuple(shape(ROWS, FEATS, dtype=BF16) for _ in range(4)),
        in_specs=specs("sshhvvvvhh"),
        out_specs=tuple(specs("vvvv")),
        scratch_shapes=[
            pltpu.VMEM((1, MSG1, FEATS), BF16),
            pltpu.VMEM((1, MSG2, FEATS), BF16),
            pltpu.VMEM(tile, F32),
            pltpu.VMEM(tile, F32),
            pltpu.VMEM((4, FEATS, BLOCK), BF16),
            pltpu.VMEM((4, FEATS, BLOCK), BF16),
            pltpu.VMEM((4, BLOCK, PAIR), F32),
            todo,
            pltpu.SemaphoreType.DMA((4,)),
        ],
        compiler_params=params(),
        cost_estimate=cost(6e9),
    )(partner, live_count, far, far2, self_a, self_v, self_g, stats, grad_a, grad_v)
    return (event_out, frame_out) + tuple(grads)


def solution(mesh):
    tokens = P("st", "hd")
    return jax.shard_map(
        on_device,
        mesh=mesh,
        in_specs=(tokens, tokens, tokens, tokens, P("st", None), P("st"), tokens, tokens),
        out_specs=(tokens,) * 6,
        check_vma=False,
    )
```

time: 308 us -> 74.5 us (0.24)
  the two profiles are of different devices: /device:TPU:258 before, /device:TPU:81 now
where the time goes in v1:
time: 74.5 us; the launch traced here: 74 us
  Pallas kernels  42.2 us (57%)
  starting transfers between devices  12.7 us (17%)
  blocking collectives  8.58 us (12%)
  local copies, waits for them, and re-layouts  8.11 us (11%)
  waiting for transfers between devices  1.46 us (2%)
  between operations  0.86 us (1%)
    pallas_call x1, Pallas kernels, on_device(): pl.pallas_call(near_backward, out_shape=(shape(ROWS, FEATS, dtype=BF16),...  13.6 us
    pallas_call x1, Pallas kernels, on_device(): pl.pallas_call(far_backward, out_shape=tuple((shape(ROWS, FEATS, dtype=BF...  10.7 us
    pallas_call x1, Pallas kernels, on_device(): pl.pallas_call(near_forward, out_shape=(shape(*wide, dtype=BF16), shape(*...  9.68 us
    psum x1, blocking collectives, on_device(): sums = lax.psum(sums, 'hd')  8.58 us
    unnamed x38, local copies, waits for them, and re-layouts  8.11 us
    pallas_call x1, Pallas kernels, on_device(): pl.pallas_call(far_forward, out_shape=(shape(*tile), shape(4, 2 * HEADS,...  7.14 us
    ppermute x1, starting transfers between devices, on_device(): far2 = lax.ppermute(msg2, 'st', outer_pairs)  5.13 us
    ppermute x1, starting transfers between devices, on_device(): far = lax.ppermute(msg, 'st', outer_pairs)  3.1 us
  transfers between devices with their start and end apart: 4, of which 1 were waited for; matrix products, arithmetic and copies ran while one was open for 0% of the time, Pallas kernels for 32%

profile of v1, /device:TPU:81, one launch (start us, length us, event | category | flops | bytes accessed | tf_op | source)
XLA Modules:
  0.0 74.0 jit_solution(2755663996864786137)
XLA Ops:
  0.6 0.0 copy-start.1
  0.6 0.9 %copy-done.1 = bf16[512,256]{1,0:T(8,128)(2,1)S(1)} copy-done((bf16[512,256]{1,0:T(8,128)(2,1)S(1)}, bf16[512,256]{1,0:T(8,128)(2,1)}, u32[]{:S(2)}) %copy-start.1) | copy-done | bytes 262168
  1.6 0.0 copy-start.2
  1.6 0.9 %copy-done.2 = bf16[512,256]{1,0:T(8,128)(2,1)S(1)} copy-done((bf16[512,256]{1,0:T(8,128)(2,1)S(1)}, bf16[512,256]{1,0:T(8,128)(2,1)}, u32[]{:S(2)}) %copy-start.2) | copy-done | bytes 262168
  2.5 0.0 copy-start.3
  2.5 0.9 %copy-done.3 = bf16[512,256]{1,0:T(8,128)(2,1)S(1)} copy-done((bf16[512,256]{1,0:T(8,128)(2,1)S(1)}, bf16[512,256]{1,0:T(8,128)(2,1)}, u32[]{:S(2)}) %copy-start.3) | copy-done | bytes 262168
  3.5 0.0 copy-start.4
  3.5 0.9 %copy-done.4 = bf16[512,256]{1,0:T(8,128)(2,1)S(1)} copy-done((bf16[512,256]{1,0:T(8,128)(2,1)S(1)}, bf16[512,256]{1,0:T(8,128)(2,1)}, u32[]{:S(2)}) %copy-start.4) | copy-done | bytes 262168
  4.4 0.0 copy-start.5
  4.4 0.7 copy-done.5
  5.1 0.0 copy-start.7
  5.1 0.7 copy-done.7
  5.8 0.0 copy-start.10
  5.8 0.0 copy-start.11
  5.8 0.6 shard_map.127.own.own1
  6.4 0.0 copy-start
  6.4 2.6 %collective-permute-start = (bf16[2064,256]{1,0:T(8,128)(2,1)S(1)}, bf16[2064,256]{1,0:T(8,128)(2,1)S(1)}, u32[]{:S(2)}, u32[]{:S(2)}) collective-permute-start(bf16[2064,256]{1,0:T(8,128)(2,1)S(1)} %shard_map.127.own.own1), channel_id=1, source_target_pairs={{0,4},{4,0},{8,12},{12,8},{16,20},{20,16},{24,28},{28,24},{32,36},... | collective-permute-start | bytes 3170312 | tf_op jit(solution)/shard_map/ppermute | solution.py:413
  9.0 3.1 %collective-permute-start.1 = (bf16[2064,256]{1,0:T(8,128)(2,1)S(1)}, bf16[2064,256]{1,0:T(8,128)(2,1)S(1)}, u32[]{:S(2)}, u32[]{:S(2)}) collective-permute-start(bf16[2064,256]{1,0:T(8,128)(2,1)S(1)} %shard_map.127.own.own1), channel_id=1, source_target_pairs={{4,8},{12,16},{20,24},{28,32},{36,40},{44,48},{52,56},{60,64},{68,... | collective-permute-start | bytes 3170312 | tf_op jit(solution)/shard_map/ppermute | solution.py:412
  12.1 0.0 collective-permute-done.near.near1
  12.1 0.0 copy-start.18
  12.2 1.0 %copy-done.18 = bf16[2064,256]{1,0:T(8,128)(2,1)} copy-done((bf16[2064,256]{1,0:T(8,128)(2,1)}, bf16[2064,256]{1,0:T(8,128)(2,1)S(1)}, u32[]{:S(2)}) %copy-start.18) | copy-done | bytes 1056792
  13.1 0.0 copy-done.10
  13.1 0.0 copy-done.11
  13.1 9.7 %shard_map.128 = (bf16[4,4,128,256]{3,2,1,0:T(8,128)(2,1)S(1)}, bf16[4,4,128,256]{3,2,1,0:T(8,128)(2,1)S(1)}, bf16[4,256,256]{2,1,0:T(8,128)(2,1)S(1)}, f32[4,8,256]{2,1,0:T(8,128)S(1)}, f32[4,256,256]{2,1,0:T(8,128)S(1)}) custom-call(s32[2,3]{1,0:T(2,128)S(1)} %copy-done.5, s32[2]{0:T(128)S(1)} %copy-done.7, bf16[2064,256]{1,0:T(8,128)(2,1)S(1)} %shard_map.127.own.own1, ...), custom_call_target="tpu_custom_call" | custom-call | flops 5000000000 | bytes 1048576 | tf_op jit(solution)/shard_map/pallas_call | solution.py:415
  22.8 0.0 copy-done
  22.8 0.0 copy-start.16
  22.8 1.0 %copy-done.16 = bf16[4,4,128,256]{3,2,1,0:T(8,128)(2,1)} copy-done((bf16[4,4,128,256]{3,2,1,0:T(8,128)(2,1)}, bf16[4,4,128,256]{3,2,1,0:T(8,128)(2,1)S(1)}, u32[]{:S(2)}) %copy-start.16) | copy-done | bytes 1048600
  23.8 0.0 copy-start.12
  23.8 0.0 copy-start.14
  23.8 1.5 %collective-permute-done.1.far.far1 = bf16[2064,256]{1,0:T(8,128)(2,1)S(1)} collective-permute-done((bf16[2064,256]{1,0:T(8,128)(2,1)S(1)}, bf16[2064,256]{1,0:T(8,128)(2,1)S(1)}, u32[]{:S(2)}, u32[]{:S(2)}) %collective-permute-start.1) | collective-permute-done | bytes 1056800 | tf_op jit(solution)/shard_map/ppermute | solution.py:412
  25.2 0.0 copy-start.9
  25.2 7.1 %shard_map.129 = (f32[4,256,256]{2,1,0:T(8,128)S(1)}, f32[4,8,256]{2,1,0:T(8,128)S(1)}, f32[8,256]{1,0:T(8,128)S(1)}) custom-call(s32[2,3]{1,0:T(2,128)S(1)} %copy-done.5, s32[2]{0:T(128)S(1)} %copy-done.7, bf16[2064,256]{1,0:T(8,128)(2,1)S(1)} %collective-permute-done.1.far.far1, bf16[4,4,128,256]{3,2,1,0:T(8,128)(2,1)S(1)} %get-tuple-element.27.self_a, ...), custom_call_target="tpu_custom_call" | custom-call | flops 3000000000 | bytes 1048576 | tf_op jit(solution)/shard_map/pallas_call | solution.py:436
  32.4 0.0 copy-done.12
  32.4 0.0 copy-done.14
  32.4 0.0 copy-done.9
  32.4 8.6 %psum.7.refs_3_ = f32[8,256]{1,0:T(8,128)S(1)} all-reduce(f32[8,256]{1,0:T(8,128)S(1)} %get-tuple-element.33), channel_id=1, replica_groups=mesh['st'=128,'hd'=4] {'hd'}, use_global_device_ids=true, to_apply=%region_0.0 | all-reduce | flops 2048 | bytes 16384 | tf_op jit(solution)/shard_map/psum | solution.py:452
  41.0 0.0 copy-start.13
  41.0 1.0 %copy-done.13 = bf16[4,256,256]{2,1,0:T(8,128)(2,1)S(1)} copy-done((bf16[4,256,256]{2,1,0:T(8,128)(2,1)S(1)}, bf16[4,256,256]{2,1,0:T(8,128)(2,1)}, u32[]{:S(2)}) %copy-start.13) | copy-done | bytes 524312
  42.0 0.0 copy-start.6
  42.0 0.0 copy-start.8
  42.0 0.4 shard_map.130
  42.5 1.9 %collective-permute-start.2 = (bf16[1152,256]{1,0:T(8,128)(2,1)S(1)}, bf16[1152,256]{1,0:T(8,128)(2,1)S(1)}, u32[]{:S(2)}, u32[]{:S(2)}) collective-permute-start(bf16[1152,256]{1,0:T(8,128)(2,1)S(1)} %get-tuple-element.34.own2), channel_id=1, source_target_pairs={{0,4},{4,0},{8,12},{12,8},{16,20},{20,16},{24,28},{28,24},{32,36},... | collective-permute-start | bytes 1769480 | tf_op jit(solution)/shard_map/ppermute | solution.py:468
  44.4 5.1 %collective-permute-start.3 = (bf16[1152,256]{1,0:T(8,128)(2,1)S(1)}, bf16[1152,256]{1,0:T(8,128)(2,1)S(1)}, u32[]{:S(2)}, u32[]{:S(2)}) collective-permute-start(bf16[1152,256]{1,0:T(8,128)(2,1)S(1)} %get-tuple-element.34.own2), channel_id=1, source_target_pairs={{4,8},{12,16},{20,24},{28,32},{36,40},{44,48},{52,56},{60,64},{68,... | collective-permute-start | bytes 1769480 | tf_op jit(solution)/shard_map/ppermute | solution.py:467
  49.5 0.0 collective-permute-done.2.near2
  49.5 0.0 copy-done.6
  49.6 0.0 copy-done.8
  49.6 0.0 copy-start.15
  49.6 0.0 copy-start.17
  49.6 13.6 %shard_map.131 = (bf16[512,256]{1,0:T(8,128)(2,1)}, bf16[512,256]{1,0:T(8,128)(2,1)}, bf16[4,4,128,256]{3,2,1,0:T(8,128)(2,1)S(1)}, f32[4,256,256]{2,1,0:T(8,128)S(1)}, f32[4,256,256]{2,1,0:T(8,128)S(1)}) custom-call(s32[2,3]{1,0:T(2,128)S(1)} %copy-done.6, s32[2]{0:T(128)S(1)} %copy-done.8, bf16[2064,256]{1,0:T(8,128)(2,1)} %copy-done, ...), custom_call_target="tpu_custom_call" | custom-call | flops 8000000000 | bytes 1048576 | tf_op jit(solution)/shard_map/pallas_call | solution.py:470
  63.2 0.0 collective-permute-done.3.far2
  63.3 0.0 copy-done.15
  63.3 0.0 copy-done.17
  63.3 10.7 %shard_map.132 = (bf16[512,256]{1,0:T(8,128)(2,1)}, bf16[512,256]{1,0:T(8,128)(2,1)}, bf16[512,256]{1,0:T(8,128)(2,1)}, bf16[512,256]{1,0:T(8,128)(2,1)}) custom-call(s32[2,3]{1,0:T(2,128)S(1)} %copy-done.6, s32[2]{0:T(128)S(1)} %copy-done.8, bf16[2064,256]{1,0:T(8,128)(2,1)} %copy-done.9, bf16[1152,256]{1,0:T(8,128)(2,1)S(1)} %collective-permute-done.3.far2, ...), custom_call_target="tpu_custom_call" | custom-call | flops 6000000000 | bytes 1048576 | tf_op jit(solution)/shard_map/pallas_call | solution.py:494
Async XLA Ops:
  0.6 1.0 %copy-start.1 = (bf16[512,256]{1,0:T(8,128)(2,1)S(1)}, bf16[512,256]{1,0:T(8,128)(2,1)}, u32[]{:S(2)}) copy-start(bf16[512,256]{1,0:T(8,128)(2,1)} %queries.1) | copy-start | bytes 786436
  1.6 0.9 %copy-start.2 = (bf16[512,256]{1,0:T(8,128)(2,1)S(1)}, bf16[512,256]{1,0:T(8,128)(2,1)}, u32[]{:S(2)}) copy-start(bf16[512,256]{1,0:T(8,128)(2,1)} %event_values.1) | copy-start | bytes 786436
  2.5 0.9 %copy-start.3 = (bf16[512,256]{1,0:T(8,128)(2,1)S(1)}, bf16[512,256]{1,0:T(8,128)(2,1)}, u32[]{:S(2)}) copy-start(bf16[512,256]{1,0:T(8,128)(2,1)} %keys.1) | copy-start | bytes 786436
  3.5 0.9 %copy-start.4 = (bf16[512,256]{1,0:T(8,128)(2,1)S(1)}, bf16[512,256]{1,0:T(8,128)(2,1)}, u32[]{:S(2)}) copy-start(bf16[512,256]{1,0:T(8,128)(2,1)} %frame_values.1) | copy-start | bytes 786436
  4.4 0.7 copy-start.5
  5.1 0.7 copy-start.7
  5.8 7.3 %copy-start.10 = (bf16[512,256]{1,0:T(8,128)(2,1)S(1)}, bf16[512,256]{1,0:T(8,128)(2,1)}, u32[]{:S(2)}) copy-start(bf16[512,256]{1,0:T(8,128)(2,1)} %event_cot.1) | copy-start | bytes 786436
  5.8 7.3 %copy-start.11 = (bf16[512,256]{1,0:T(8,128)(2,1)S(1)}, bf16[512,256]{1,0:T(8,128)(2,1)}, u32[]{:S(2)}) copy-start(bf16[512,256]{1,0:T(8,128)(2,1)} %frame_cot.1) | copy-start | bytes 786436
  6.4 16.4 %copy-start = (bf16[2064,256]{1,0:T(8,128)(2,1)}, bf16[2064,256]{1,0:T(8,128)(2,1)S(1)}, u32[]{:S(2)}) copy-start(bf16[2064,256]{1,0:T(8,128)(2,1)S(1)} %shard_map.127.own.own1) | copy-start | bytes 3170308
  6.4 5.7 %collective-permute-start = (bf16[2064,256]{1,0:T(8,128)(2,1)S(1)}, bf16[2064,256]{1,0:T(8,128)(2,1)S(1)}, u32[]{:S(2)}, u32[]{:S(2)}) collective-permute-start(bf16[2064,256]{1,0:T(8,128)(2,1)S(1)} %shard_map.127.own.own1), channel_id=1, source_target_pairs={{0,4},{4,0},{8,12},{12,8},{16,20},{20,16},{24,28},{28,24},{32,36},... | collective-permute-start | bytes 3170312 | tf_op jit(solution)/shard_map/ppermute | solution.py:413
  9.0 16.2 %collective-permute-start.1 = (bf16[2064,256]{1,0:T(8,128)(2,1)S(1)}, bf16[2064,256]{1,0:T(8,128)(2,1)S(1)}, u32[]{:S(2)}, u32[]{:S(2)}) collective-permute-start(bf16[2064,256]{1,0:T(8,128)(2,1)S(1)} %shard_map.127.own.own1), channel_id=1, source_target_pairs={{4,8},{12,16},{20,24},{28,32},{36,40},{44,48},{52,56},{60,64},{68,... | collective-permute-start | bytes 3170312 | tf_op jit(solution)/shard_map/ppermute | solution.py:412
  12.1 1.0 %copy-start.18 = (bf16[2064,256]{1,0:T(8,128)(2,1)}, bf16[2064,256]{1,0:T(8,128)(2,1)S(1)}, u32[]{:S(2)}) copy-start(bf16[2064,256]{1,0:T(8,128)(2,1)S(1)} %collective-permute-done.near.near1) | copy-start | bytes 3170308
  22.8 1.0 %copy-start.16 = (bf16[4,4,128,256]{3,2,1,0:T(8,128)(2,1)}, bf16[4,4,128,256]{3,2,1,0:T(8,128)(2,1)S(1)}, u32[]{:S(2)}) copy-start(bf16[4,4,128,256]{3,2,1,0:T(8,128)(2,1)S(1)} %get-tuple-element.35.self_v) | copy-start | bytes 3145732
  23.8 8.6 %copy-start.12 = (bf16[4,256,256]{2,1,0:T(8,128)(2,1)}, bf16[4,256,256]{2,1,0:T(8,128)(2,1)S(1)}, u32[]{:S(2)}) copy-start(bf16[4,256,256]{2,1,0:T(8,128)(2,1)S(1)} %get-tuple-element.28.cot_t.refs_1_) | copy-start | bytes 1572868
  23.8 8.6 %copy-start.14 = (bf16[4,4,128,256]{3,2,1,0:T(8,128)(2,1)}, bf16[4,4,128,256]{3,2,1,0:T(8,128)(2,1)S(1)}, u32[]{:S(2)}) copy-start(bf16[4,4,128,256]{3,2,1,0:T(8,128)(2,1)S(1)} %get-tuple-element.27.self_a) | copy-start | bytes 3145732
  25.2 7.2 %copy-start.9 = (bf16[2064,256]{1,0:T(8,128)(2,1)}, bf16[2064,256]{1,0:T(8,128)(2,1)S(1)}, u32[]{:S(2)}) copy-start(bf16[2064,256]{1,0:T(8,128)(2,1)S(1)} %collective-permute-done.1.far.far1) | copy-start | bytes 3170308
  41.0 1.0 %copy-start.13 = (bf16[4,256,256]{2,1,0:T(8,128)(2,1)S(1)}, bf16[4,256,256]{2,1,0:T(8,128)(2,1)}, u32[]{:S(2)}) copy-start(bf16[4,256,256]{2,1,0:T(8,128)(2,1)} %copy-done.12) | copy-start | bytes 1572868
  42.0 7.5 %copy-start.6 = (s32[2,3]{1,0:T(2,128)S(1)}, s32[2,3]{1,0:T(2,128)}, u32[]{:S(2)}) copy-start(s32[2,3]{1,0:T(2,128)} %partner.9) | copy-start | bytes 76
  42.0 7.5 %copy-start.8 = (s32[2]{0:T(128)S(1)}, s32[2]{0:T(128)}, u32[]{:S(2)}) copy-start(s32[2]{0:T(128)} %live.9) | copy-start | bytes 28
  42.5 7.1 %collective-permute-start.2 = (bf16[1152,256]{1,0:T(8,128)(2,1)S(1)}, bf16[1152,256]{1,0:T(8,128)(2,1)S(1)}, u32[]{:S(2)}, u32[]{:S(2)}) collective-permute-start(bf16[1152,256]{1,0:T(8,128)(2,1)S(1)} %get-tuple-element.34.own2), channel_id=1, source_target_pairs={{0,4},{4,0},{8,12},{12,8},{16,20},{20,16},{24,28},{28,24},{32,36},... | collective-permute-start | bytes 1769480 | tf_op jit(solution)/shard_map/ppermute | solution.py:468
  44.4 18.8 %collective-permute-start.3 = (bf16[1152,256]{1,0:T(8,128)(2,1)S(1)}, bf16[1152,256]{1,0:T(8,128)(2,1)S(1)}, u32[]{:S(2)}, u32[]{:S(2)}) collective-permute-start(bf16[1152,256]{1,0:T(8,128)(2,1)S(1)} %get-tuple-element.34.own2), channel_id=1, source_target_pairs={{4,8},{12,16},{20,24},{28,32},{36,40},{44,48},{52,56},{60,64},{68,... | collective-permute-start | bytes 1769480 | tf_op jit(solution)/shard_map/ppermute | solution.py:467
  49.6 13.7 %copy-start.15 = (bf16[4,4,128,256]{3,2,1,0:T(8,128)(2,1)S(1)}, bf16[4,4,128,256]{3,2,1,0:T(8,128)(2,1)}, u32[]{:S(2)}) copy-start(bf16[4,4,128,256]{3,2,1,0:T(8,128)(2,1)} %copy-done.14) | copy-start | bytes 3145732
  49.6 13.7 %copy-start.17 = (bf16[4,4,128,256]{3,2,1,0:T(8,128)(2,1)S(1)}, bf16[4,4,128,256]{3,2,1,0:T(8,128)(2,1)}, u32[]{:S(2)}) copy-start(bf16[4,4,128,256]{3,2,1,0:T(8,128)(2,1)} %copy-done.16) | copy-start | bytes 3145732

commit v2 on v1

v2 whole, which is shorter than its diff:
```python
import jax
import jax.numpy as jnp
from jax import lax
from jax.experimental import pallas as pl
from jax.experimental.pallas import tpu as pltpu
from jax.sharding import PartitionSpec as P

DH = 64
BLOCK = 256
SLOTS = 3
HEADS = 4
FEATS = HEADS * DH
ROWS = 2 * BLOCK
PAIR = 2 * DH
EPS = 1e-06
NEG = -1e30
LOG2E = 1.4426950408889634
SCALE = DH**-0.5

KEYS, FVALS, QUERIES, EVALS, CODES = 0, ROWS, 2 * ROWS, 3 * ROWS, 4 * ROWS
MSG1 = 4 * ROWS + 16
FAR1 = MSG1 + 16
STATS = 2 * ROWS
MSG2 = 2 * ROWS + 4 * 32
FAR2 = MSG2 + 16

F32 = jnp.float32
BF16 = jnp.bfloat16
VMEM_LIMIT = 32 * 1024 * 1024
PACK_LIMIT = 62 * 1024 * 1024


def dot(a, b):
    return jnp.dot(a, b, preferred_element_type=F32)


def dot_other_way(a, b):
    return lax.dot_general(a, b, (((1,), (1,)), ((), ())), preferred_element_type=F32)


def params(limit=VMEM_LIMIT, **more):
    return pltpu.CompilerParams(vmem_limit_bytes=limit, **more)


def cost(flops):
    return pl.CostEstimate(flops=int(flops), bytes_accessed=1 << 10, transcendentals=0)


def lanes(head):
    return slice((head // 2) * PAIR, (head // 2 + 1) * PAIR)


def feats(head):
    return slice(head * DH, (head + 1) * DH)


def stacked(parts):
    return jnp.concatenate(parts, axis=0)


def start_all(*copies):
    made = [pltpu.make_async_copy(*c) for c in copies]
    for c in made:
        c.start()
    return made


def code_for(partner, live, run):
    code = jnp.int32(0)
    for a in range(2):
        for s in range(SLOTS):
            block = partner[a, s] - 2 * run
            hit = (s < live[a]) & (block >= 0) & (block < 2)
            code += jnp.where(hit, jnp.left_shift(1, 2 * a + jnp.clip(block, 0, 1)), 0)
    return code


def bits(code):
    return [
        (a, f, jnp.bitwise_and(jnp.right_shift(code, 2 * a + f), 1)) for a in range(2) for f in range(2)
    ]


def pair_list(todo, as_events, as_frames):
    count = jnp.int32(0)
    for a, f, hit in bits(as_events):
        todo[count] = a * 2 + f
        count += hit
    for a, f, hit in bits(as_frames):
        todo[count] = (2 + f) * 2 + a
        count += hit
    return count


def read_code(msg, half):
    part = msg[CODES:MSG1, half * PAIR : (half + 1) * PAIR].astype(F32)
    return jnp.max(part).astype(jnp.int32)


def masked(features_first, head):
    tile = features_first[lanes(head), :]
    row = lax.broadcasted_iota(jnp.int32, tile.shape, 0)
    return jnp.where(row // DH == head % 2, tile, jnp.zeros_like(tile))


def pack_kernel(partner_in, live_in, queries, event_values, keys, frame_values, near, far, plan, partner, live, sems):
    parts = ((keys, KEYS), (frame_values, FVALS), (queries, QUERIES), (event_values, EVALS))
    tables = start_all((partner_in, partner, sems.at[0]), (live_in, live, sems.at[1]))
    arrays = start_all(*((part, far.at[low : low + ROWS], sems.at[2 + i]) for i, (part, low) in enumerate(parts)))
    for c in tables:
        c.wait()
    run = lax.axis_index("st")
    odd = lax.rem(run, 2)
    plan[0] = code_for(partner, live, run)
    for half, target in enumerate((run + 1 - 2 * odd, run - 1 + 2 * odd)):
        code = code_for(partner, live, target)
        plan[1 + half] = code
        far[CODES:FAR1, half * PAIR : (half + 1) * PAIR] = jnp.full(
            (32, PAIR), code.astype(F32), F32
        ).astype(BF16)
    for c in arrays:
        c.wait()
    near[...] = far[0:MSG1, :]


def attend(msg, vals_t, self_a, soft, acc, ahead, todo, count):
    def place(n):
        entry = todo[n]
        me = lax.div(entry, 2)
        side = lax.div(me, 2)
        block = lax.rem(entry, 2)
        return me, side * 2 + block, pl.multiple_of(side * (2 * ROWS) + block * BLOCK, BLOCK)

    def scores_of(n):
        me, _, row = place(n)
        return [dot(msg[pl.ds(row, BLOCK), lanes(h)], self_a[me, h]) for h in range(HEADS)]

    def keep(scores):
        for h in range(HEADS):
            ahead[h] = scores[h]

    keep(scores_of(0))

    def pair(n, _):
        me, at, _ = place(n)
        old, whole = soft[me], acc[me]
        scores = [ahead[h] for h in range(HEADS)]
        following = scores_of(jnp.minimum(n + 1, jnp.maximum(count - 1, 0)))
        tops, totals, decays, weights = [], [], [], []
        for h in range(HEADS):
            top = jnp.maximum(old[h : h + 1], jnp.max(scores[h], axis=0, keepdims=True))
            decay = jnp.exp(old[h : h + 1] - top)
            expo = jnp.exp(scores[h] - top)
            tops.append(top)
            decays.append(decay)
            totals.append(old[HEADS + h : HEADS + h + 1] * decay + jnp.sum(expo, axis=0, keepdims=True))
            weights.append(expo.astype(BF16))
        acc[me] = stacked(
            [whole[feats(h)] * decays[h] + dot(vals_t[at, feats(h), :], weights[h]) for h in range(HEADS)]
        )
        soft[me] = stacked(tops + totals)
        keep(following)
        return 0

    lax.fori_loop(0, count, pair, 0)


def other_values(msg, vals_t):
    for side, base in ((0, FVALS), (1, EVALS)):
        for block in range(2):
            low = base + block * BLOCK
            vals_t[side * 2 + block] = msg[low : low + BLOCK, :].T


def other_queries(msg, a_t):
    for side, base in ((0, KEYS), (1, QUERIES)):
        for block in range(2):
            low = base + block * BLOCK
            a_t[side * 2 + block] = msg[low : low + BLOCK, :].T * BF16(SCALE)


def near_forward(
    plan,
    own,
    near,
    event_cot,
    frame_cot,
    self_a,
    self_v,
    cot_t,
    soft,
    acc,
    near_a_t,
    cots,
    own_vals,
    near_vals,
    ahead,
    todo,
    sems,
):
    fetched = start_all((event_cot, cots.at[0], sems.at[0]), (frame_cot, cots.at[1], sems.at[1]))
    for side, (base_a, base_v) in enumerate(((QUERIES, EVALS), (KEYS, FVALS))):
        for block in range(2):
            me = side * 2 + block
            low = block * BLOCK
            a_t = own[base_a + low : base_a + low + BLOCK, :].T * BF16(SCALE)
            v_t = own[base_v + low : base_v + low + BLOCK, :].T
            own_vals[(1 - side) * 2 + block] = v_t
            for h in range(HEADS):
                self_a[me, h] = masked(a_t, h)
                self_v[me, h] = masked(v_t, h)
            soft[me, 0:HEADS, :] = jnp.full((HEADS, BLOCK), NEG, F32)
            soft[me, HEADS : 2 * HEADS, :] = jnp.zeros((HEADS, BLOCK), F32)
            acc[me] = jnp.zeros((FEATS, BLOCK), F32)
    count = pair_list(todo, plan[0], plan[0])
    attend(own, own_vals, self_a, soft, acc, ahead, todo, count)
    other_values(near, near_vals)
    count = pair_list(todo, plan[1], read_code(near, 0))
    attend(near, near_vals, self_a, soft, acc, ahead, todo, count)
    other_queries(near, near_a_t)
    for c in fetched:
        c.wait()
    for me in range(4):
        low = (me % 2) * BLOCK
        cot_t[me] = cots[me // 2, low : low + BLOCK, :].T


def far_forward(plan, far, self_a, cot_t, soft_in, acc_in, att, lse, sums, soft, vals_t, ahead, todo):
    acc = att
    soft[...] = soft_in[...]
    acc[...] = acc_in[...]
    other_values(far, vals_t)
    count = pair_list(todo, plan[2], read_code(far, 1))
    attend(far, vals_t, self_a, soft, acc, ahead, todo, count)
    for me in range(4):
        old, whole = soft[me], acc[me]
        total = old[HEADS : 2 * HEADS]
        lse[me] = stacked([old[0:HEADS] * LOG2E + jnp.log2(total), jnp.zeros((HEADS, BLOCK), F32)])
        inverse = 1.0 / total
        values = stacked([whole[feats(h)] * inverse[h : h + 1] for h in range(HEADS)])
        att[me] = values
        square = jnp.sum(values * values, axis=0, keepdims=True)
        slope = jnp.sum(values * cot_t[me].astype(F32), axis=0, keepdims=True)
        for to in range(sums.shape[0]):
            sums[to, 2 * me : 2 * me + 1, :] = square
            sums[to, 2 * me + 1 : 2 * me + 2, :] = slope


def split(value):
    high = value.astype(BF16).astype(F32)
    rest = value - high
    middle = rest.astype(BF16).astype(F32)
    return high, middle, rest - middle


def grad_kernel(width, att, cot_t, lse, sums, grad_t, normed_t, stats, msg, far):
    whole = jnp.sum(sums[...], axis=0)
    for me in range(4):
        rms = lax.rsqrt(whole[2 * me : 2 * me + 1, :] / width + EPS)
        slope = rms * whole[2 * me + 1 : 2 * me + 2, :] / width
        values = att[me]
        normed = values * rms
        grad = (rms * (cot_t[me].astype(F32) - normed * slope)).astype(BF16)
        grad_t[me] = grad
        normed_t[me] = normed.astype(BF16)
        side, block = 1 - me // 2, me % 2
        low = side * ROWS + block * BLOCK
        turned = grad.T
        msg[low : low + BLOCK, :] = turned
        far[low : low + BLOCK, :] = turned
        product = grad.astype(F32) * values
        deltas = [jnp.sum(product[feats(h)], axis=0, keepdims=True) for h in range(HEADS)]
        mine = stacked([lse[me, 0:HEADS, :]] + deltas)
        stats[me] = mine
        at = STATS + 32 * (2 * side + block)
        rows = stacked(split(mine) + (jnp.zeros_like(mine),)).astype(BF16)
        msg[at : at + 32, :] = rows
        far[at : at + 32, :] = rows
    far[MSG2:FAR2, :] = jnp.zeros((16, FEATS), BF16)


def as_columns(rows):
    return stacked([rows, jnp.zeros((PAIR - 2 * HEADS, BLOCK), F32)]).T


def other_grads(msg, g_t, columns):
    for side in range(2):
        for block in range(2):
            low = side * ROWS + block * BLOCK
            g_t[side * 2 + block] = msg[low : low + BLOCK, :].T
            low = STATS + 32 * (side * 2 + block)
            rows = msg[low : low + 32, :].astype(F32)
            columns[side * 2 + block] = as_columns(rows[0:8] + rows[8:16] + rows[16:24])


def in_order(dots, weigh, outs):
    dots(0)
    dots(1)
    dots(2)
    weigh(0)
    dots(3)
    for h in range(HEADS):
        outs(h)
        if h + 1 < HEADS:
            weigh(h + 1)


def slopes(made, row_stats, columns, h):
    scores, self_change, other_change = made
    scores = scores * LOG2E
    self_p = jnp.exp2(scores - row_stats[h : h + 1])
    other_p = jnp.exp2(scores - columns[:, h : h + 1])
    g = HEADS + h
    slope = self_p * (self_change - row_stats[g : g + 1]) + other_p * (other_change - columns[:, g : g + 1])
    return slope.astype(BF16), self_p.astype(BF16), other_p.astype(BF16)


def back(msg1, msg2, a_t, g_t, columns, self_a, self_v, self_g, stats, grad_a, grad_v, todo, count):
    def pair(n, _):
        entry = todo[n]
        me = lax.div(entry, 2)
        side = lax.div(me, 2)
        block = lax.rem(entry, 2)
        row_a = pl.multiple_of(side * (2 * ROWS) + block * BLOCK, BLOCK)
        row_v = pl.multiple_of(side * (2 * ROWS) + ROWS + block * BLOCK, BLOCK)
        row_g = pl.multiple_of(side * ROWS + block * BLOCK, BLOCK)
        at = side * 2 + block
        mine, theirs = stats[me], columns[at]
        made, ready, sums = {}, {}, {}

        def dots(h):
            made[h] = (
                dot(msg1[pl.ds(row_a, BLOCK), lanes(h)], self_a[me, h]),
                dot(msg1[pl.ds(row_v, BLOCK), lanes(h)], self_g[me, h]),
                dot(msg2[pl.ds(row_g, BLOCK), lanes(h)], self_v[me, h]),
            )

        def weigh(h):
            ready[h] = slopes(made[h], mine, theirs, h)

        def outs(h):
            slope, _, other_p = ready[h]
            sums[h] = dot(a_t[at, feats(h), :], slope), dot(g_t[at, feats(h), :], other_p)

        in_order(dots, weigh, outs)
        grad_a[me] += stacked([sums[h][0] for h in range(HEADS)])
        grad_v[me] += stacked([sums[h][1] for h in range(HEADS)])
        return 0

    lax.fori_loop(0, count, pair, 0)


def back_own(msg1, msg2, columns, self_a, self_v, self_g, grad_t, stats, grad_a, grad_v, todo, count):
    def pair(n, _):
        entry = todo[n]
        me = lax.div(entry, 2)
        block = lax.rem(entry, 2)
        frame = 2 + block
        row_a = pl.multiple_of(KEYS + block * BLOCK, BLOCK)
        row_v = pl.multiple_of(FVALS + block * BLOCK, BLOCK)
        row_g = pl.multiple_of(block * BLOCK, BLOCK)
        mine, theirs = stats[me], columns[block]
        made, ready, sums = {}, {}, {}

        def dots(h):
            made[h] = (
                dot(msg1[pl.ds(row_a, BLOCK), lanes(h)], self_a[me, h]),
                dot(msg1[pl.ds(row_v, BLOCK), lanes(h)], self_g[me, h]),
                dot(msg2[pl.ds(row_g, BLOCK), lanes(h)], self_v[me, h]),
            )

        def weigh(h):
            ready[h] = slopes(made[h], mine, theirs, h)

        def outs(h):
            slope, self_p, other_p = ready[h]
            half = slice((h % 2) * DH, (h % 2 + 1) * DH)
            sums[h] = (
                dot(self_a[frame, h, half, :], slope),
                dot(grad_t[frame, feats(h), :], other_p),
                dot_other_way(self_a[me, h, half, :], slope),
                dot_other_way(grad_t[me, feats(h), :], self_p),
            )

        in_order(dots, weigh, outs)
        grad_a[me] += stacked([sums[h][0] for h in range(HEADS)])
        grad_v[me] += stacked([sums[h][1] for h in range(HEADS)])
        grad_a[frame] += stacked([sums[h][2] for h in range(HEADS)])
        grad_v[frame] += stacked([sums[h][3] for h in range(HEADS)])
        return 0

    lax.fori_loop(0, count, pair, 0)


def own_backward(
    plan, own1, own2, self_a, self_v, grad_t, stats, self_g, grad_a, grad_v, columns, todo
):
    for me in range(4):
        for h in range(HEADS):
            self_g[me, h] = masked(grad_t[me], h)
        grad_a[me] = jnp.zeros((FEATS, BLOCK), F32)
        grad_v[me] = jnp.zeros((FEATS, BLOCK), F32)
    for block in range(2):
        columns[block] = as_columns(stats[2 + block])
    count = pair_list(todo, plan[0], jnp.int32(0))
    back_own(own1, own2, columns, self_a, self_v, self_g, grad_t, stats, grad_a, grad_v, todo, count)


def send_grads(me, grad_a, grad_v, ready, outs, sems):
    side, low = me // 2, (me % 2) * BLOCK
    copies = []
    for k, grad in enumerate((grad_a, grad_v)):
        ready[2 * me + k] = grad[me].astype(BF16).T
        copies += start_all((ready.at[2 * me + k], outs[2 * side + k].at[low : low + BLOCK], sems.at[2 * me + k]))
    return copies


def near_backward(
    plan,
    near1,
    far1,
    near2,
    self_a,
    self_v,
    self_g,
    near_a_t,
    normed_t,
    stats,
    grad_a_in,
    grad_v_in,
    grad_a,
    grad_v,
    event_out,
    frame_out,
    grad_queries,
    grad_event_values,
    grad_keys,
    grad_frame_values,
    far_a_t,
    g_t,
    columns,
    ready,
    todo,
    sems,
):
    grad_a[...] = grad_a_in[...]
    grad_v[...] = grad_v_in[...]
    other_grads(near2, g_t, columns)
    count = pair_list(todo, plan[1], read_code(near1, 0))
    back(near1, near2, near_a_t, g_t, columns, self_a, self_v, self_g, stats, grad_a, grad_v, todo, count)
    outs = (grad_queries, grad_event_values, grad_keys, grad_frame_values)
    copies = []
    for me in range(4):
        copies += send_grads(me, grad_a, grad_v, ready, outs, sems)
        low = (me % 2) * BLOCK
        ready[8 + me] = normed_t[me].T
        copies += start_all(
            (ready.at[8 + me], (event_out, frame_out)[me // 2].at[low : low + BLOCK], sems.at[8 + me])
        )
    other_queries(far1, far_a_t)
    for c in copies:
        c.wait()


def far_backward(
    plan,
    far1,
    far2,
    self_a,
    self_v,
    self_g,
    far_a_t,
    stats,
    grad_a_in,
    grad_v_in,
    _queries,
    _event_values,
    _keys,
    _frame_values,
    grad_queries,
    grad_event_values,
    grad_keys,
    grad_frame_values,
    grad_a,
    grad_v,
    g_t,
    columns,
    ready,
    todo,
    sems,
):
    code = read_code(far1, 1)
    touched = [jnp.bitwise_and(plan[2], 3 * 4**a) != 0 for a in range(2)] + [
        jnp.bitwise_and(code, 5 * 2**f) != 0 for f in range(2)
    ]
    outs = (grad_queries, grad_event_values, grad_keys, grad_frame_values)
    count = pair_list(todo, plan[2], code)

    @pl.when(count > 0)
    def _():
        for me in range(4):

            @pl.when(touched[me])
            def _():
                grad_a[me] = grad_a_in[me]
                grad_v[me] = grad_v_in[me]

        other_grads(far2, g_t, columns)
        back(far1, far2, far_a_t, g_t, columns, self_a, self_v, self_g, stats, grad_a, grad_v, todo, count)
        for me in range(4):

            @pl.when(touched[me])
            def _():
                send_grads(me, grad_a, grad_v, ready, outs, sems)

        for me in range(4):

            @pl.when(touched[me])
            def _():
                side, low = me // 2, (me % 2) * BLOCK
                for k in range(2):
                    pltpu.make_async_copy(
                        ready.at[2 * me + k], outs[2 * side + k].at[low : low + BLOCK], sems.at[2 * me + k]
                    ).wait()


def shape(*dims, dtype=F32):
    return jax.ShapeDtypeStruct(dims, dtype)


def specs(kinds):
    space = {"s": pltpu.SMEM, "v": pltpu.VMEM, "h": pltpu.HBM}
    return [pl.BlockSpec(memory_space=space[k]) for k in kinds]


def kernel(body, operands, places, outs, out_places, scratch=(), flops=0, limit=VMEM_LIMIT, aliases=()):
    return pl.pallas_call(
        body,
        out_shape=tuple(outs),
        in_specs=specs(places),
        out_specs=tuple(specs(out_places)),
        scratch_shapes=list(scratch),
        compiler_params=params(limit),
        cost_estimate=cost(flops),
        input_output_aliases=dict(aliases),
    )(*operands)


def on_device(
    event_queries,
    event_values,
    frame_keys,
    frame_values,
    partner,
    live_count,
    event_cotangent,
    frame_cotangent,
):
    width = FEATS * lax.axis_size("hd")
    runs = lax.axis_size("st")
    inner_pairs = [(i, i ^ 1) for i in range(runs)]
    outer_pairs = [(i, i + 1) for i in range(1, runs - 1, 2)] + [(i + 1, i) for i in range(1, runs - 1, 2)]
    tile = (4, FEATS, BLOCK)
    wide = (4, HEADS, PAIR, BLOCK)
    small = (4, 2 * HEADS, BLOCK)
    todo = pltpu.SMEM((16,), jnp.int32)

    msg1, far_msg1, plan = kernel(
        pack_kernel,
        (partner, live_count, event_queries, event_values, frame_keys, frame_values),
        "hhhhhh",
        (shape(MSG1, FEATS, dtype=BF16), shape(FAR1, FEATS, dtype=BF16), shape(8, dtype=jnp.int32)),
        "vvs",
        [
            pltpu.SMEM((2, SLOTS), jnp.int32),
            pltpu.SMEM((2,), jnp.int32),
            pltpu.SemaphoreType.DMA((6,)),
        ],
        limit=PACK_LIMIT,
    )
    far1 = lax.ppermute(far_msg1, "st", outer_pairs)
    near1 = lax.ppermute(msg1, "st", inner_pairs)

    self_a, self_v, cot_t, soft, acc, near_a_t = kernel(
        near_forward,
        (plan, msg1, near1, event_cotangent, frame_cotangent),
        "svvhh",
        (
            shape(*wide, dtype=BF16),
            shape(*wide, dtype=BF16),
            shape(*tile, dtype=BF16),
            shape(*small),
            shape(*tile),
            shape(*tile, dtype=BF16),
        ),
        "vvvvvv",
        [
            pltpu.VMEM((2, ROWS, FEATS), BF16),
            pltpu.VMEM(tile, BF16),
            pltpu.VMEM(tile, BF16),
            pltpu.VMEM((HEADS, BLOCK, BLOCK), F32),
            todo,
            pltpu.SemaphoreType.DMA((2,)),
        ],
        1e6,
    )
    att, lse, sums = kernel(
        far_forward,
        (plan, far1, self_a, cot_t, soft, acc),
        "svvvvv",
        (shape(*tile), shape(*small), shape(lax.axis_size("hd"), 8, BLOCK)),
        "vvv",
        [
            pltpu.VMEM(small, F32),
            pltpu.VMEM(tile, BF16),
            pltpu.VMEM((HEADS, BLOCK, BLOCK), F32),
            todo,
        ],
        1e6,
    )
    sums = lax.all_to_all(sums, "hd", 0, 0)

    grad_t, normed_t, stats, msg2, far_msg2 = kernel(
        lambda *refs: grad_kernel(width, *refs),
        (att, cot_t, lse, sums),
        "vvvv",
        (
            shape(*tile, dtype=BF16),
            shape(*tile, dtype=BF16),
            shape(*small),
            shape(MSG2, FEATS, dtype=BF16),
            shape(FAR2, FEATS, dtype=BF16),
        ),
        "vvvvv",
        flops=1e6,
    )
    far2 = lax.ppermute(far_msg2, "st", outer_pairs)
    near2 = lax.ppermute(msg2, "st", inner_pairs)

    self_g, grad_a, grad_v = kernel(
        own_backward,
        (plan, msg1, msg2, self_a, self_v, grad_t, stats),
        "svvvvvv",
        (shape(*wide, dtype=BF16), shape(*tile), shape(*tile)),
        "vvv",
        [pltpu.VMEM((2, BLOCK, PAIR), F32), todo],
        1e6,
    )
    whole = [shape(ROWS, FEATS, dtype=BF16)]
    grad_a, grad_v, event_out, frame_out, *grads, far_a_t = kernel(
        near_backward,
        (plan, near1, far1, near2, self_a, self_v, self_g, near_a_t, normed_t, stats, grad_a, grad_v),
        "svvvvvvvvvvv",
        [shape(*tile)] * 2 + whole * 6 + [shape(*tile, dtype=BF16)],
        "vvhhhhhhv",
        [
            pltpu.VMEM(tile, BF16),
            pltpu.VMEM((4, BLOCK, PAIR), F32),
            pltpu.VMEM((12, BLOCK, FEATS), BF16),
            todo,
            pltpu.SemaphoreType.DMA((12,)),
        ],
        1e6,
    )
    grads = kernel(
        far_backward,
        (plan, far1, far2, self_a, self_v, self_g, far_a_t, stats, grad_a, grad_v, *grads),
        "svvvvvvvvvhhhh",
        whole * 4,
        "hhhh",
        [
            pltpu.VMEM(tile, F32),
            pltpu.VMEM(tile, F32),
            pltpu.VMEM(tile, BF16),
            pltpu.VMEM((4, BLOCK, PAIR), F32),
            pltpu.VMEM((8, BLOCK, FEATS), BF16),
            todo,
            pltpu.SemaphoreType.DMA((8,)),
        ],
        1e6,
        aliases=((10, 0), (11, 1), (12, 2), (13, 3)),
    )
    return (event_out, frame_out) + tuple(grads)


def solution(mesh):
    tokens = P("st", "hd")
    return jax.shard_map(
        on_device,
        mesh=mesh,
        in_specs=(tokens, tokens, tokens, tokens, P("st", None), P("st"), tokens, tokens),
        out_specs=(tokens,) * 6,
        check_vma=False,
    )
```

time: 74.5 us -> 55.6 us (0.75)
  the two profiles are of different devices: /device:TPU:81 before, /device:TPU:281 now
where the time goes in v2:
time: 55.6 us; the launch traced here: 55.3 us
  Pallas kernels  25.6 us (46%)
  starting transfers between devices  15.1 us (27%)
  blocking collectives  8.24 us (15%)
  waiting for transfers between devices  3.61 us (6%)
  local copies, waits for them, and re-layouts  1.9 us (3%)
  between operations  0.77 us (1%)
    pallas_call x7, Pallas kernels, kernel(): pl.pallas_call(body, out_shape=tuple(outs), in_specs=specs(places), out_s...  25.6 us
    all_to_all x1, blocking collectives, on_device(): sums = lax.all_to_all(sums, 'hd', 0, 0)  8.24 us
    ppermute x1, starting transfers between devices, on_device(): far2 = lax.ppermute(far_msg2, 'st', outer_pairs)  6.29 us
    ppermute x1, starting transfers between devices, on_device(): far1 = lax.ppermute(far_msg1, 'st', outer_pairs)  4.98 us
    ppermute x1, waiting for transfers between devices, on_device(): near1 = lax.ppermute(msg1, 'st', inner_pairs)  2.85 us
    ppermute x1, starting transfers between devices, on_device(): near2 = lax.ppermute(msg2, 'st', inner_pairs)  1.92 us
    ppermute x1, starting transfers between devices, on_device(): near1 = lax.ppermute(msg1, 'st', inner_pairs)  1.92 us
    unnamed x12, local copies, waits for them, and re-layouts  1.9 us
  transfers between devices with their start and end apart: 4, of which 2 were waited for; matrix products, arithmetic and copies ran while one was open for 0% of the time, Pallas kernels for 25%

profile of v2, /device:TPU:281, one launch (start us, length us, event | category | flops | bytes accessed | tf_op | source)
XLA Modules:
  0.0 55.3 jit_solution(971862583304930518)
XLA Ops:
  0.6 0.0 copy-start.3
  0.6 0.0 copy-start.2
  0.7 2.7 %shard_map.127 = (bf16[2064,256]{1,0:T(8,128)(2,1)}, bf16[2080,256]{1,0:T(8,128)(2,1)}, s32[8]{0:T(128)}) custom-call(s32[2,3]{1,0:T(2,128)} %partner_in.1, s32[2]{0:T(128)} %live_in.1, bf16[512,256]{1,0:T(8,128)(2,1)} %queries.1, bf16[512,256]{1,0:T(8,128)(2,1)} %event_values.1, bf16[512,256]{1,0:T(8,128)(2,1)} %keys.1, bf16[512,256]{1,0:T(8,128)(2,1)} %frame_values.1), custom_call_target="tpu_custom_call" | custom-call | bytes 1024 | tf_op jit(solution)/shard_map/pallas_call | solution.py:537
  3.3 5.0 %collective-permute-start.1 = (bf16[2080,256]{1,0:T(8,128)(2,1)}, bf16[2080,256]{1,0:T(8,128)(2,1)S(1)}, u32[]{:S(2)}, u32[]{:S(2)}) collective-permute-start(bf16[2080,256]{1,0:T(8,128)(2,1)} %get-tuple-element.41), channel_id=1, source_target_pairs={{4,8},{12,16},{20,24},{28,32},{36,40},{44,48},{52,56},{60,64},{68,... | collective-permute-start | bytes 3194888 | tf_op jit(solution)/shard_map/ppermute | solution.py:581
  8.3 1.9 %collective-permute-start = (bf16[2064,256]{1,0:T(8,128)(2,1)}, bf16[2064,256]{1,0:T(8,128)(2,1)S(1)}, u32[]{:S(2)}, u32[]{:S(2)}) collective-permute-start(bf16[2064,256]{1,0:T(8,128)(2,1)} %get-tuple-element.40.own.own1), channel_id=1, source_target_pairs={{0,4},{4,0},{8,12},{12,8},{16,20},{20,16},{24,28},{28,24},{32,36},... | collective-permute-start | bytes 3170312 | tf_op jit(solution)/shard_map/ppermute | solution.py:582
  10.2 2.8 %collective-permute-done.near.near1 = bf16[2064,256]{1,0:T(8,128)(2,1)S(1)} collective-permute-done((bf16[2064,256]{1,0:T(8,128)(2,1)}, bf16[2064,256]{1,0:T(8,128)(2,1)S(1)}, u32[]{:S(2)}, u32[]{:S(2)}) %collective-permute-start) | collective-permute-done | bytes 1056800 | tf_op jit(solution)/shard_map/ppermute | solution.py:582
  13.1 0.0 copy-done.3
  13.1 0.0 copy-done.2
  13.1 0.0 copy-start
  13.1 1.2 %copy-done = bf16[2064,256]{1,0:T(8,128)(2,1)S(1)} copy-done((bf16[2064,256]{1,0:T(8,128)(2,1)S(1)}, bf16[2064,256]{1,0:T(8,128)(2,1)}, u32[]{:S(2)}) %copy-start) | copy-done | bytes 1056792
  14.3 0.0 copy-start.4
  14.3 0.7 %copy-done.4 = s32[8]{0:T(128)S(1)} copy-done((s32[8]{0:T(128)S(1)}, s32[8]{0:T(128)}, u32[]{:S(2)}) %copy-start.4) | copy-done | bytes 56
  15.0 5.4 %shard_map.128 = (bf16[4,4,128,256]{3,2,1,0:T(8,128)(2,1)S(1)}, bf16[4,4,128,256]{3,2,1,0:T(8,128)(2,1)S(1)}, bf16[4,256,256]{2,1,0:T(8,128)(2,1)S(1)}, f32[4,8,...) custom-call(s32[8]{0:T(128)S(1)} %copy-done.4, bf16[2064,256]{1,0:T(8,128)(2,1)S(1)} %copy-done, ...), custom_call_target="tpu_custom_call" | custom-call | flops 1000000 | bytes 1024 | tf_op jit(solution)/shard_map/pallas_call | solution.py:537
  20.4 0.8 %collective-permute-done.1.far.far1 = bf16[2080,256]{1,0:T(8,128)(2,1)S(1)} collective-permute-done((bf16[2080,256]{1,0:T(8,128)(2,1)}, bf16[2080,256]{1,0:T(8,128)(2,1)S(1)}, u32[]{:S(2)}, u32[]{:S(2)}) %collective-permute-start.1) | collective-permute-done | bytes 1064992 | tf_op jit(solution)/shard_map/ppermute | solution.py:581
  21.2 2.9 %shard_map.129 = (f32[4,256,256]{2,1,0:T(8,128)S(1)}, f32[4,8,256]{2,1,0:T(8,128)S(1)}, f32[4,8,256]{2,1,0:T(8,128)S(1)}) custom-call(s32[8]{0:T(128)S(1)} %copy-done.4, bf16[2080,256]{1,0:T(8,128)(2,1)S(1)} %collective-permute-done.1.far.far1, bf16[4,4,128,256]{3,2,1,0:T(8,128)(2,1)S(1)} %get-tuple-element.42.self_a, ...), custom_call_target="tpu_custom_call" | custom-call | flops 1000000 | bytes 1024 | tf_op jit(solution)/shard_map/pallas_call | solution.py:537
  24.1 0.0 copy-start.1
  24.1 0.0 copy-start.5
  24.1 8.2 %all_to_all.5.refs_3_ = f32[4,8,256]{2,1,0:T(8,128)S(1)} all-to-all(f32[4,8,256]{2,1,0:T(8,128)S(1)} %get-tuple-element.48), channel_id=1, replica_groups=mesh['st'=128,'hd'=4] {'hd'}, dimensions={0} | all-to-all | bytes 65536 | tf_op jit(solution)/shard_map/all_to_all | solution.py:621
  32.4 0.4 shard_map.130
  32.8 6.3 %collective-permute-start.3 = (bf16[1168,256]{1,0:T(8,128)(2,1)S(1)}, bf16[1168,256]{1,0:T(8,128)(2,1)S(1)}, u32[]{:S(2)}, u32[]{:S(2)}) collective-permute-start(bf16[1168,256]{1,0:T(8,128)(2,1)S(1)} %get-tuple-element.60), channel_id=1, source_target_pairs={{4,8},{12,16},{20,24},{28,32},{36,40},{44,48},{52,56},{60,64},{68,... | collective-permute-start | bytes 1794056 | tf_op jit(solution)/shard_map/ppermute | solution.py:637
  39.1 1.9 %collective-permute-start.2 = (bf16[1152,256]{1,0:T(8,128)(2,1)S(1)}, bf16[1152,256]{1,0:T(8,128)(2,1)S(1)}, u32[]{:S(2)}, u32[]{:S(2)}) collective-permute-start(bf16[1152,256]{1,0:T(8,128)(2,1)S(1)} %get-tuple-element.49.own2), channel_id=1, source_target_pairs={{0,4},{4,0},{8,12},{12,8},{16,20},{20,16},{24,28},{28,24},{32,36},... | collective-permute-start | bytes 1769480 | tf_op jit(solution)/shard_map/ppermute | solution.py:638
  41.0 0.0 copy-done.1
  41.0 0.0 copy-done.5
  41.0 4.3 %shard_map.131 = (bf16[4,4,128,256]{3,2,1,0:T(8,128)(2,1)S(1)}, f32[4,256,256]{2,1,0:T(8,128)S(1)}, f32[4,256,256]{2,1,0:T(8,128)S(1)}) custom-call(s32[8]{0:T(128)S(1)} %copy-done.5, bf16[2064,256]{1,0:T(8,128)(2,1)S(1)} %copy-done.1, bf16[1152,256]{1,0:T(8,128)(2,1)S(1)} %get-tuple-element.49.own2, bf16[4,4,128,256]{3,2,1,0:T(8,128)(2,1)S(1)} %get-tuple-element.42.self_a, ...), custom_call_target="tpu_custom_call" | custom-call | flops 1000000 | bytes 1024 | tf_op jit(solution)/shard_map/pallas_call | solution.py:537
  45.4 0.0 collective-permute-done.2.near2
  45.4 4.0 %shard_map.132 = (f32[4,256,256]{2,1,0:T(8,128)S(1)}, f32[4,256,256]{2,1,0:T(8,128)S(1)}, bf16[512,256]{1,0:T(8,128)(2,1)}, bf16[512,256]{1,0:T(8,128)(2,1)}, bf...) custom-call(s32[8]{0:T(128)S(1)} %copy-done.5, ...), custom_call_target="tpu_custom_call" | custom-call | flops 1000000 | bytes 1024 | tf_op jit(solution)/shard_map/pallas_call | solution.py:537
  49.4 0.0 collective-permute-done.3.far2
  49.4 5.8 %shard_map.133 = (bf16[512,256]{1,0:T(8,128)(2,1)}, bf16[512,256]{1,0:T(8,128)(2,1)}, bf16[512,256]{1,0:T(8,128)(2,1)}, bf16[512,256]{1,0:T(8,128)(2,1)}) custom-call(s32[8]{0:T(128)S(1)} %copy-done.5, bf16[2080,256]{1,0:T(8,128)(2,1)S(1)} %collective-permute-done.1.far.far1, ...), custom_call_target="tpu_custom_call", output_to_operand_aliasing={{0}: (10, {}), {1}: (11, {}), {2}: (12, {}), {3}: (13, {})} | custom-call | flops 1000000 | bytes 1024 | tf_op jit(solution)/shard_map/pallas_call | solution.py:537
Async XLA Ops:
  0.6 12.4 %copy-start.3 = (bf16[512,256]{1,0:T(8,128)(2,1)S(1)}, bf16[512,256]{1,0:T(8,128)(2,1)}, u32[]{:S(2)}) copy-start(bf16[512,256]{1,0:T(8,128)(2,1)} %frame_cot.1) | copy-start | bytes 786436
  0.6 12.4 %copy-start.2 = (bf16[512,256]{1,0:T(8,128)(2,1)S(1)}, bf16[512,256]{1,0:T(8,128)(2,1)}, u32[]{:S(2)}) copy-start(bf16[512,256]{1,0:T(8,128)(2,1)} %event_cot.1) | copy-start | bytes 786436
  3.3 17.8 %collective-permute-start.1 = (bf16[2080,256]{1,0:T(8,128)(2,1)}, bf16[2080,256]{1,0:T(8,128)(2,1)S(1)}, u32[]{:S(2)}, u32[]{:S(2)}) collective-permute-start(bf16[2080,256]{1,0:T(8,128)(2,1)} %get-tuple-element.41), channel_id=1, source_target_pairs={{4,8},{12,16},{20,24},{28,32},{36,40},{44,48},{52,56},{60,64},{68,... | collective-permute-start | bytes 3194888 | tf_op jit(solution)/shard_map/ppermute | solution.py:581
  8.3 4.8 %collective-permute-start = (bf16[2064,256]{1,0:T(8,128)(2,1)}, bf16[2064,256]{1,0:T(8,128)(2,1)S(1)}, u32[]{:S(2)}, u32[]{:S(2)}) collective-permute-start(bf16[2064,256]{1,0:T(8,128)(2,1)} %get-tuple-element.40.own.own1), channel_id=1, source_target_pairs={{0,4},{4,0},{8,12},{12,8},{16,20},{20,16},{24,28},{28,24},{32,36},... | collective-permute-start | bytes 3170312 | tf_op jit(solution)/shard_map/ppermute | solution.py:582
  13.1 1.2 %copy-start = (bf16[2064,256]{1,0:T(8,128)(2,1)S(1)}, bf16[2064,256]{1,0:T(8,128)(2,1)}, u32[]{:S(2)}) copy-start(bf16[2064,256]{1,0:T(8,128)(2,1)} %get-tuple-element.40.own.own1) | copy-start | bytes 3170308
  14.3 0.7 %copy-start.4 = (s32[8]{0:T(128)S(1)}, s32[8]{0:T(128)}, u32[]{:S(2)}) copy-start(s32[8]{0:T(128)} %get-tuple-element.39.plan) | copy-start | bytes 100
  24.1 16.9 %copy-start.1 = (bf16[2064,256]{1,0:T(8,128)(2,1)S(1)}, bf16[2064,256]{1,0:T(8,128)(2,1)}, u32[]{:S(2)}) copy-start(bf16[2064,256]{1,0:T(8,128)(2,1)} %get-tuple-element.40.own.own1) | copy-start | bytes 3170308
  24.1 16.9 %copy-start.5 = (s32[8]{0:T(128)S(1)}, s32[8]{0:T(128)}, u32[]{:S(2)}) copy-start(s32[8]{0:T(128)} %get-tuple-element.39.plan) | copy-start | bytes 100
  32.8 16.6 %collective-permute-start.3 = (bf16[1168,256]{1,0:T(8,128)(2,1)S(1)}, bf16[1168,256]{1,0:T(8,128)(2,1)S(1)}, u32[]{:S(2)}, u32[]{:S(2)}) collective-permute-start(bf16[1168,256]{1,0:T(8,128)(2,1)S(1)} %get-tuple-element.60), channel_id=1, source_target_pairs={{4,8},{12,16},{20,24},{28,32},{36,40},{44,48},{52,56},{60,64},{68,... | collective-permute-start | bytes 1794056 | tf_op jit(solution)/shard_map/ppermute | solution.py:637
  39.1 6.3 %collective-permute-start.2 = (bf16[1152,256]{1,0:T(8,128)(2,1)S(1)}, bf16[1152,256]{1,0:T(8,128)(2,1)S(1)}, u32[]{:S(2)}, u32[]{:S(2)}) collective-permute-start(bf16[1152,256]{1,0:T(8,128)(2,1)S(1)} %get-tuple-element.49.own2), channel_id=1, source_target_pairs={{0,4},{4,0},{8,12},{12,8},{16,20},{20,16},{24,28},{28,24},{32,36},... | collective-permute-start | bytes 1769480 | tf_op jit(solution)/shard_map/ppermute | solution.py:638

commit v3 on v2

--- a/solution.py
+++ b/solution.py
@@ -23,6 +23,7 @@
 STATS = 2 * ROWS
 MSG2 = 2 * ROWS + 4 * 32
 FAR2 = MSG2 + 16
+KEPT = 3
 
 F32 = jnp.float32
 BF16 = jnp.bfloat16
@@ -103,10 +104,10 @@
     return jnp.where(row // DH == head % 2, tile, jnp.zeros_like(tile))
 
 
-def pack_kernel(partner_in, live_in, queries, event_values, keys, frame_values, near, far, plan, partner, live, sems):
+def pack_kernel(partner_in, live_in, queries, event_values, keys, frame_values, msg, plan, partner, live, sems):
     parts = ((keys, KEYS), (frame_values, FVALS), (queries, QUERIES), (event_values, EVALS))
     tables = start_all((partner_in, partner, sems.at[0]), (live_in, live, sems.at[1]))
-    arrays = start_all(*((part, far.at[low : low + ROWS], sems.at[2 + i]) for i, (part, low) in enumerate(parts)))
+    arrays = start_all(*((part, msg.at[low : low + ROWS], sems.at[2 + i]) for i, (part, low) in enumerate(parts)))
     for c in tables:
         c.wait()
     run = lax.axis_index("st")
@@ -115,12 +116,9 @@
     for half, target in enumerate((run + 1 - 2 * odd, run - 1 + 2 * odd)):
         code = code_for(partner, live, target)
         plan[1 + half] = code
-        far[CODES:FAR1, half * PAIR : (half + 1) * PAIR] = jnp.full(
-            (32, PAIR), code.astype(F32), F32
-        ).astype(BF16)
+        msg[CODES:FAR1, half * PAIR : (half + 1) * PAIR] = jnp.full((32, PAIR), code.astype(F32), F32).astype(BF16)
     for c in arrays:
         c.wait()
-    near[...] = far[0:MSG1, :]
 
 
 def attend(msg, vals_t, self_a, soft, acc, ahead, todo, count):
@@ -315,7 +313,7 @@
     return slope.astype(BF16), self_p.astype(BF16), other_p.astype(BF16)
 
 
-def back(msg1, msg2, a_t, g_t, columns, self_a, self_v, self_g, stats, grad_a, grad_v, todo, count):
+def back(msg1, msg2, a_t, g_t, columns, self_a, self_v, self_g, stats, grad_a, grad_v, todo, count, first=0):
     def pair(n, _):
         entry = todo[n]
         me = lax.div(entry, 2)
@@ -340,6 +338,58 @@
 
         def outs(h):
             slope, _, other_p = ready[h]
+            sums[h] = dot(a_t[at, feats(h), :], slope), dot(g_t[at, feats(h), :], other_p)
+
+        in_order(dots, weigh, outs)
+        grad_a[me] += stacked([sums[h][0] for h in range(HEADS)])
+        grad_v[me] += stacked([sums[h][1] for h in range(HEADS)])
+        return 0
+
+    lax.fori_loop(first, count, pair, 0)
+
+
+def part_way(msg1, self_a, self_g, stats, kept_scores, kept_terms, todo, count):
+    def pair(n, _):
+        entry = todo[n]
+        me = lax.div(entry, 2)
+        side = lax.div(me, 2)
+        block = lax.rem(entry, 2)
+        row_a = pl.multiple_of(side * (2 * ROWS) + block * BLOCK, BLOCK)
+        row_v = pl.multiple_of(side * (2 * ROWS) + ROWS + block * BLOCK, BLOCK)
+        mine = stats[me]
+        scores = [dot(msg1[pl.ds(row_a, BLOCK), lanes(h)], self_a[me, h]) * LOG2E for h in range(HEADS)]
+        changes = [dot(msg1[pl.ds(row_v, BLOCK), lanes(h)], self_g[me, h]) for h in range(HEADS)]
+        for h in range(HEADS):
+            g = HEADS + h
+            kept_scores[n, h] = scores[h]
+            kept_terms[n, h] = jnp.exp2(scores[h] - mine[h : h + 1]) * (changes[h] - mine[g : g + 1])
+        return 0
+
+    lax.fori_loop(0, count, pair, 0)
+
+
+def back_rest(msg2, a_t, g_t, columns, self_v, kept_scores, kept_terms, grad_a, grad_v, todo, count):
+    def pair(n, _):
+        entry = todo[n]
+        me = lax.div(entry, 2)
+        side = lax.div(me, 2)
+        block = lax.rem(entry, 2)
+        row_g = pl.multiple_of(side * ROWS + block * BLOCK, BLOCK)
+        at = side * 2 + block
+        theirs = columns[at]
+        made, ready, sums = {}, {}, {}
+
+        def dots(h):
+            made[h] = dot(msg2[pl.ds(row_g, BLOCK), lanes(h)], self_v[me, h])
+
+        def weigh(h):
+            g = HEADS + h
+            other_p = jnp.exp2(kept_scores[n, h] - theirs[:, h : h + 1])
+            slope = kept_terms[n, h] + other_p * (made[h] - theirs[:, g : g + 1])
+            ready[h] = slope.astype(BF16), other_p.astype(BF16)
+
+        def outs(h):
+            slope, other_p = ready[h]
             sums[h] = dot(a_t[at, feats(h), :], slope), dot(g_t[at, feats(h), :], other_p)
 
         in_order(dots, weigh, outs)
@@ -437,6 +487,8 @@
     grad_keys,
     grad_frame_values,
     far_a_t,
+    kept_scores,
+    kept_terms,
     g_t,
     columns,
     ready,
@@ -458,6 +510,8 @@
             (ready.at[8 + me], (event_out, frame_out)[me // 2].at[low : low + BLOCK], sems.at[8 + me])
         )
     other_queries(far1, far_a_t)
+    count = pair_list(todo, plan[2], read_code(far1, 1))
+    part_way(far1, self_a, self_g, stats, kept_scores, kept_terms, todo, jnp.minimum(count, KEPT))
     for c in copies:
         c.wait()
 
@@ -471,6 +525,8 @@
     self_g,
     far_a_t,
     stats,
+    kept_scores,
+    kept_terms,
     grad_a_in,
     grad_v_in,
     _queries,
@@ -506,7 +562,11 @@
                 grad_v[me] = grad_v_in[me]
 
         other_grads(far2, g_t, columns)
-        back(far1, far2, far_a_t, g_t, columns, self_a, self_v, self_g, stats, grad_a, grad_v, todo, count)
+        begun = jnp.minimum(count, KEPT)
+        back_rest(far2, far_a_t, g_t, columns, self_v, kept_scores, kept_terms, grad_a, grad_v, todo, begun)
+        back(
+            far1, far2, far_a_t, g_t, columns, self_a, self_v, self_g, stats, grad_a, grad_v, todo, count, begun
+        )
         for me in range(4):
 
             @pl.when(touched[me])
@@ -565,12 +625,12 @@
     small = (4, 2 * HEADS, BLOCK)
     todo = pltpu.SMEM((16,), jnp.int32)
 
-    msg1, far_msg1, plan = kernel(
+    far_msg1, plan = kernel(
         pack_kernel,
         (partner, live_count, event_queries, event_values, frame_keys, frame_values),
         "hhhhhh",
-        (shape(MSG1, FEATS, dtype=BF16), shape(FAR1, FEATS, dtype=BF16), shape(8, dtype=jnp.int32)),
-        "vvs",
+        (shape(FAR1, FEATS, dtype=BF16), shape(8, dtype=jnp.int32)),
+        "vs",
         [
             pltpu.SMEM((2, SLOTS), jnp.int32),
             pltpu.SMEM((2,), jnp.int32),
@@ -579,6 +639,7 @@
         limit=PACK_LIMIT,
     )
     far1 = lax.ppermute(far_msg1, "st", outer_pairs)
+    msg1 = far_msg1[0:MSG1]
     near1 = lax.ppermute(msg1, "st", inner_pairs)
 
     self_a, self_v, cot_t, soft, acc, near_a_t = kernel(
@@ -647,12 +708,12 @@
         1e6,
     )
     whole = [shape(ROWS, FEATS, dtype=BF16)]
-    grad_a, grad_v, event_out, frame_out, *grads, far_a_t = kernel(
+    grad_a, grad_v, event_out, frame_out, *grads, far_a_t, kept_scores, kept_terms = kernel(
         near_backward,
         (plan, near1, far1, near2, self_a, self_v, self_g, near_a_t, normed_t, stats, grad_a, grad_v),
         "svvvvvvvvvvv",
-        [shape(*tile)] * 2 + whole * 6 + [shape(*tile, dtype=BF16)],
-        "vvhhhhhhv",
+        [shape(*tile)] * 2 + whole * 6 + [shape(*tile, dtype=BF16)] + [shape(KEPT, HEADS, BLOCK, BLOCK)] * 2,
+        "vvhhhhhhvvv",
         [
             pltpu.VMEM(tile, BF16),
             pltpu.VMEM((4, BLOCK, PAIR), F32),
@@ -664,8 +725,8 @@
     )
     grads = kernel(
         far_backward,
-        (plan, far1, far2, self_a, self_v, self_g, far_a_t, stats, grad_a, grad_v, *grads),
-        "svvvvvvvvvhhhh",
+        (plan, far1, far2, self_a, self_v, self_g, far_a_t, stats, kept_scores, kept_terms, grad_a, grad_v, *grads),
+        "svvvvvvvvvvvhhhh",
         whole * 4,
         "hhhh",
         [
@@ -678,7 +739,7 @@
             pltpu.SemaphoreType.DMA((8,)),
         ],
         1e6,
-        aliases=((10, 0), (11, 1), (12, 2), (13, 3)),
+        aliases=((12, 0), (13, 1), (14, 2), (15, 3)),
     )
     return (event_out, frame_out) + tuple(grads)
 

time: 55.6 us -> 54.9 us (0.987)
  the two profiles are of different devices: /device:TPU:281 before, /device:TPU:249 now
where the time goes in v3:
time: 54.9 us; the launch traced here: 54.6 us
  Pallas kernels  22.9 us (42%)
  starting transfers between devices  15.3 us (28%)
  blocking collectives  8.12 us (15%)
  waiting for transfers between devices  6.2 us (11%)
  local copies, waits for them, and re-layouts  1.33 us (2%)
  between operations  0.75 us (1%)
    pallas_call x7, Pallas kernels, kernel(): pl.pallas_call(body, out_shape=tuple(outs), in_specs=specs(places), out_s...  22.9 us
    all_to_all x1, blocking collectives, on_device(): sums = lax.all_to_all(sums, 'hd', 0, 0)  8.12 us
    ppermute x1, starting transfers between devices, on_device(): far2 = lax.ppermute(far_msg2, 'st', outer_pairs)  6.4 us
    ppermute x1, starting transfers between devices, on_device(): far1 = lax.ppermute(far_msg1, 'st', outer_pairs)  5.11 us
    ppermute x1, waiting for transfers between devices, on_device(): far1 = lax.ppermute(far_msg1, 'st', outer_pairs)  3.55 us
    ppermute x1, waiting for transfers between devices, on_device(): near1 = lax.ppermute(msg1, 'st', inner_pairs)  2.64 us
    ppermute x1, starting transfers between devices, on_device(): near1 = lax.ppermute(msg1, 'st', inner_pairs)  1.92 us
    ppermute x1, starting transfers between devices, on_device(): near2 = lax.ppermute(msg2, 'st', inner_pairs)  1.92 us
  transfers between devices with their start and end apart: 4, of which 2 were waited for; matrix products, arithmetic and copies ran while one was open for 2% of the time, Pallas kernels for 27%

profile of v3, /device:TPU:249, one launch (start us, length us, event | category | flops | bytes accessed | tf_op | source)
XLA Modules:
  0.0 54.6 jit_solution(7074057126703524280)
XLA Ops:
  0.6 2.2 %shard_map.127 = (bf16[2080,256]{1,0:T(8,128)(2,1)}, s32[8]{0:T(128)}) custom-call(s32[2,3]{1,0:T(2,128)} %partner_in.1, s32[2]{0:T(128)} %live_in.1, bf16[512,256]{1,0:T(8,128)(2,1)} %queries.1, bf16[512,256]{1,0:T(8,128)(2,1)} %event_values.1, bf16[512,256]{1,0:T(8,128)(2,1)} %keys.1, bf16[512,256]{1,0:T(8,128)(2,1)} %frame_values.1), custom_call_target="tpu_custom_call" | custom-call | bytes 1024 | tf_op jit(solution)/shard_map/pallas_call | solution.py:597
  2.9 0.0 copy-start
  2.9 0.0 copy-start.1
  2.9 0.0 copy-start.2
  2.9 5.1 %collective-permute-start.1 = (bf16[2080,256]{1,0:T(8,128)(2,1)}, bf16[2080,256]{1,0:T(8,128)(2,1)S(1)}, u32[]{:S(2)}, u32[]{:S(2)}) collective-permute-start(bf16[2080,256]{1,0:T(8,128)(2,1)} %get-tuple-element.41), channel_id=1, source_target_pairs={{4,8},{12,16},{20,24},{28,32},{36,40},{44,48},{52,56},{60,64},{68,... | collective-permute-start | bytes 3194888 | tf_op jit(solution)/shard_map/ppermute | solution.py:641
  8.0 1.3 %slice.3.own.own1 = bf16[2064,256]{1,0:T(8,128)(2,1)S(1)} slice(bf16[2080,256]{1,0:T(8,128)(2,1)} %get-tuple-element.41), slice={[0:2064], [0:256]} | slice | bytes 2113536 | tf_op jit(solution)/shard_map/slice | solution.py:642
  9.3 1.9 %collective-permute-start = (bf16[2064,256]{1,0:T(8,128)(2,1)S(1)}, bf16[2064,256]{1,0:T(8,128)(2,1)S(1)}, u32[]{:S(2)}, u32[]{:S(2)}) collective-permute-start(bf16[2064,256]{1,0:T(8,128)(2,1)S(1)} %slice.3.own.own1), channel_id=1, source_target_pairs={{0,4},{4,0},{8,12},{12,8},{16,20},{20,16},{24,28},{28,24},{32,36},... | collective-permute-start | bytes 3170312 | tf_op jit(solution)/shard_map/ppermute | solution.py:643
  11.3 2.6 %collective-permute-done.near.near1 = bf16[2064,256]{1,0:T(8,128)(2,1)S(1)} collective-permute-done((bf16[2064,256]{1,0:T(8,128)(2,1)S(1)}, bf16[2064,256]{1,0:T(8,128)(2,1)S(1)}, u32[]{:S(2)}, u32[]{:S(2)}) %collective-permute-start) | collective-permute-done | bytes 1056800 | tf_op jit(solution)/shard_map/ppermute | solution.py:643
  13.9 0.0 copy-done
  13.9 0.0 copy-done.1
  13.9 0.0 copy-done.2
  13.9 5.4 %shard_map.128 = (bf16[4,4,128,256]{3,2,1,0:T(8,128)(2,1)S(1)}, bf16[4,4,128,256]{3,2,1,0:T(8,128)(2,1)S(1)}, bf16[4,256,256]{2,1,0:T(8,128)(2,1)S(1)}, f32[4,8,...) custom-call(s32[8]{0:T(128)S(1)} %copy-done.2, ...), custom_call_target="tpu_custom_call" | custom-call | flops 1000000 | bytes 1024 | tf_op jit(solution)/shard_map/pallas_call | solution.py:597
  19.3 3.6 %collective-permute-done.1.far.far1 = bf16[2080,256]{1,0:T(8,128)(2,1)S(1)} collective-permute-done((bf16[2080,256]{1,0:T(8,128)(2,1)}, bf16[2080,256]{1,0:T(8,128)(2,1)S(1)}, u32[]{:S(2)}, u32[]{:S(2)}) %collective-permute-start.1) | collective-permute-done | bytes 1064992 | tf_op jit(solution)/shard_map/ppermute | solution.py:641
  22.9 2.1 %shard_map.129 = (f32[4,256,256]{2,1,0:T(8,128)S(1)}, f32[4,8,256]{2,1,0:T(8,128)S(1)}, f32[4,8,256]{2,1,0:T(8,128)S(1)}) custom-call(s32[8]{0:T(128)S(1)} %copy-done.2, bf16[2080,256]{1,0:T(8,128)(2,1)S(1)} %collective-permute-done.1.far.far1, bf16[4,4,128,256]{3,2,1,0:T(8,128)(2,1)S(1)} %get-tuple-element.42.self_a, ...), custom_call_target="tpu_custom_call" | custom-call | flops 1000000 | bytes 1024 | tf_op jit(solution)/shard_map/pallas_call | solution.py:597
  24.9 8.1 %all_to_all.5.refs_3_ = f32[4,8,256]{2,1,0:T(8,128)S(1)} all-to-all(f32[4,8,256]{2,1,0:T(8,128)S(1)} %get-tuple-element.48), channel_id=1, replica_groups=mesh['st'=128,'hd'=4] {'hd'}, dimensions={0} | all-to-all | bytes 65536 | tf_op jit(solution)/shard_map/all_to_all | solution.py:682
  33.1 0.4 shard_map.130
  33.5 6.4 %collective-permute-start.3 = (bf16[1168,256]{1,0:T(8,128)(2,1)S(1)}, bf16[1168,256]{1,0:T(8,128)(2,1)S(1)}, u32[]{:S(2)}, u32[]{:S(2)}) collective-permute-start(bf16[1168,256]{1,0:T(8,128)(2,1)S(1)} %get-tuple-element.60), channel_id=1, source_target_pairs={{4,8},{12,16},{20,24},{28,32},{36,40},{44,48},{52,56},{60,64},{68,... | collective-permute-start | bytes 1794056 | tf_op jit(solution)/shard_map/ppermute | solution.py:698
  39.9 1.9 %collective-permute-start.2 = (bf16[1152,256]{1,0:T(8,128)(2,1)S(1)}, bf16[1152,256]{1,0:T(8,128)(2,1)S(1)}, u32[]{:S(2)}, u32[]{:S(2)}) collective-permute-start(bf16[1152,256]{1,0:T(8,128)(2,1)S(1)} %get-tuple-element.49.own2), channel_id=1, source_target_pairs={{0,4},{4,0},{8,12},{12,8},{16,20},{20,16},{24,28},{28,24},{32,36},... | collective-permute-start | bytes 1769480 | tf_op jit(solution)/shard_map/ppermute | solution.py:699
  41.8 3.2 %shard_map.131 = (bf16[4,4,128,256]{3,2,1,0:T(8,128)(2,1)S(1)}, f32[4,256,256]{2,1,0:T(8,128)S(1)}, f32[4,256,256]{2,1,0:T(8,128)S(1)}) custom-call(s32[8]{0:T(128)S(1)} %copy-done.2, bf16[2064,256]{1,0:T(8,128)(2,1)S(1)} %slice.3.own.own1, bf16[1152,256]{1,0:T(8,128)(2,1)S(1)} %get-tuple-element.49.own2, ...), custom_call_target="tpu_custom_call" | custom-call | flops 1000000 | bytes 1024 | tf_op jit(solution)/shard_map/pallas_call | solution.py:597
  45.0 0.0 collective-permute-done.2.near2
  45.0 6.1 %shard_map.132 = (f32[4,256,256]{2,1,0:T(8,128)S(1)}, f32[4,256,256]{2,1,0:T(8,128)S(1)}, bf16[512,256]{1,0:T(8,128)(2,1)}, bf16[512,256]{1,0:T(8,128)(2,1)}, bf...) custom-call(s32[8]{0:T(128)S(1)} %copy-done.2, ...), custom_call_target="tpu_custom_call" | custom-call | flops 1000000 | bytes 1024 | tf_op jit(solution)/shard_map/pallas_call | solution.py:597
  51.1 0.0 collective-permute-done.3.far2
  51.1 3.5 %shard_map.133 = (bf16[512,256]{1,0:T(8,128)(2,1)}, bf16[512,256]{1,0:T(8,128)(2,1)}, bf16[512,256]{1,0:T(8,128)(2,1)}, bf16[512,256]{1,0:T(8,128)(2,1)}) custom-call(s32[8]{0:T(128)S(1)} %copy-done.2, bf16[2080,256]{1,0:T(8,128)(2,1)S(1)} %collective-permute-done.1.far.far1, ...), custom_call_target="tpu_custom_call", output_to_operand_aliasing={{0}: (12, {}), {1}: (13, {}), {2}: (14, {}), {3}: (15, {})} | custom-call | flops 1000000 | bytes 1024 | tf_op jit(solution)/shard_map/pallas_call | solution.py:597
Async XLA Ops:
  2.9 11.0 %copy-start = (bf16[512,256]{1,0:T(8,128)(2,1)S(1)}, bf16[512,256]{1,0:T(8,128)(2,1)}, u32[]{:S(2)}) copy-start(bf16[512,256]{1,0:T(8,128)(2,1)} %event_cot.1) | copy-start | bytes 786436
  2.9 11.0 %copy-start.1 = (bf16[512,256]{1,0:T(8,128)(2,1)S(1)}, bf16[512,256]{1,0:T(8,128)(2,1)}, u32[]{:S(2)}) copy-start(bf16[512,256]{1,0:T(8,128)(2,1)} %frame_cot.1) | copy-start | bytes 786436
  2.9 11.0 %copy-start.2 = (s32[8]{0:T(128)S(1)}, s32[8]{0:T(128)}, u32[]{:S(2)}) copy-start(s32[8]{0:T(128)} %get-tuple-element.40.plan) | copy-start | bytes 100
  2.9 20.0 %collective-permute-start.1 = (bf16[2080,256]{1,0:T(8,128)(2,1)}, bf16[2080,256]{1,0:T(8,128)(2,1)S(1)}, u32[]{:S(2)}, u32[]{:S(2)}) collective-permute-start(bf16[2080,256]{1,0:T(8,128)(2,1)} %get-tuple-element.41), channel_id=1, source_target_pairs={{4,8},{12,16},{20,24},{28,32},{36,40},{44,48},{52,56},{60,64},{68,... | collective-permute-start | bytes 3194888 | tf_op jit(solution)/shard_map/ppermute | solution.py:641
  9.3 4.6 %collective-permute-start = (bf16[2064,256]{1,0:T(8,128)(2,1)S(1)}, bf16[2064,256]{1,0:T(8,128)(2,1)S(1)}, u32[]{:S(2)}, u32[]{:S(2)}) collective-permute-start(bf16[2064,256]{1,0:T(8,128)(2,1)S(1)} %slice.3.own.own1), channel_id=1, source_target_pairs={{0,4},{4,0},{8,12},{12,8},{16,20},{20,16},{24,28},{28,24},{32,36},... | collective-permute-start | bytes 3170312 | tf_op jit(solution)/shard_map/ppermute | solution.py:643
  33.5 17.6 %collective-permute-start.3 = (bf16[1168,256]{1,0:T(8,128)(2,1)S(1)}, bf16[1168,256]{1,0:T(8,128)(2,1)S(1)}, u32[]{:S(2)}, u32[]{:S(2)}) collective-permute-start(bf16[1168,256]{1,0:T(8,128)(2,1)S(1)} %get-tuple-element.60), channel_id=1, source_target_pairs={{4,8},{12,16},{20,24},{28,32},{36,40},{44,48},{52,56},{60,64},{68,... | collective-permute-start | bytes 1794056 | tf_op jit(solution)/shard_map/ppermute | solution.py:698
  39.9 5.1 %collective-permute-start.2 = (bf16[1152,256]{1,0:T(8,128)(2,1)S(1)}, bf16[1152,256]{1,0:T(8,128)(2,1)S(1)}, u32[]{:S(2)}, u32[]{:S(2)}) collective-permute-start(bf16[1152,256]{1,0:T(8,128)(2,1)S(1)} %get-tuple-element.49.own2), channel_id=1, source_target_pairs={{0,4},{4,0},{8,12},{12,8},{16,20},{20,16},{24,28},{28,24},{32,36},... | collective-permute-start | bytes 1769480 | tf_op jit(solution)/shard_map/ppermute | solution.py:699

commit v4 on v3

--- a/solution.py
+++ b/solution.py
@@ -21,13 +21,16 @@
 MSG1 = 4 * ROWS + 16
 FAR1 = MSG1 + 16
 STATS = 2 * ROWS
-MSG2 = 2 * ROWS + 4 * 32
+MIDDLE = STATS + 4 * 8
+LOW = MIDDLE + 4 * 8
+MSG2 = LOW + 4 * 4
 FAR2 = MSG2 + 16
 KEPT = 3
+HELD = 4
 
 F32 = jnp.float32
 BF16 = jnp.bfloat16
-VMEM_LIMIT = 32 * 1024 * 1024
+VMEM_LIMIT = 28 * 1024 * 1024
 PACK_LIMIT = 62 * 1024 * 1024
 
 
@@ -122,6 +125,8 @@
 
 
 def attend(msg, vals_t, self_a, soft, acc, ahead, todo, count):
+    slots = ahead.shape[0]
+
     def place(n):
         entry = todo[n]
         me = lax.div(entry, 2)
@@ -133,17 +138,20 @@
         me, _, row = place(n)
         return [dot(msg[pl.ds(row, BLOCK), lanes(h)], self_a[me, h]) for h in range(HEADS)]
 
-    def keep(scores):
+    def keep(n, scores):
+        slot = jnp.minimum(n, slots - 1)
         for h in range(HEADS):
-            ahead[h] = scores[h]
-
-    keep(scores_of(0))
+            ahead[slot, h] = scores[h]
+
+    keep(0, scores_of(0))
 
     def pair(n, _):
         me, at, _ = place(n)
         old, whole = soft[me], acc[me]
-        scores = [ahead[h] for h in range(HEADS)]
-        following = scores_of(jnp.minimum(n + 1, jnp.maximum(count - 1, 0)))
+        slot = jnp.minimum(n, slots - 1)
+        scores = [ahead[slot, h] for h in range(HEADS)]
+        after = jnp.minimum(n + 1, count - 1)
+        following = scores_of(after)
         tops, totals, decays, weights = [], [], [], []
         for h in range(HEADS):
             top = jnp.maximum(old[h : h + 1], jnp.max(scores[h], axis=0, keepdims=True))
@@ -157,7 +165,7 @@
             [whole[feats(h)] * decays[h] + dot(vals_t[at, feats(h), :], weights[h]) for h in range(HEADS)]
         )
         soft[me] = stacked(tops + totals)
-        keep(following)
+        keep(after, following)
         return 0
 
     lax.fori_loop(0, count, pair, 0)
@@ -189,10 +197,11 @@
     soft,
     acc,
     near_a_t,
+    own_scores,
+    near_scores,
     cots,
     own_vals,
     near_vals,
-    ahead,
     todo,
     sems,
 ):
@@ -211,10 +220,10 @@
             soft[me, HEADS : 2 * HEADS, :] = jnp.zeros((HEADS, BLOCK), F32)
             acc[me] = jnp.zeros((FEATS, BLOCK), F32)
     count = pair_list(todo, plan[0], plan[0])
-    attend(own, own_vals, self_a, soft, acc, ahead, todo, count)
+    attend(own, own_vals, self_a, soft, acc, own_scores, todo, count)
     other_values(near, near_vals)
     count = pair_list(todo, plan[1], read_code(near, 0))
-    attend(near, near_vals, self_a, soft, acc, ahead, todo, count)
+    attend(near, near_vals, self_a, soft, acc, near_scores, todo, count)
     other_queries(near, near_a_t)
     for c in fetched:
         c.wait()
@@ -253,6 +262,7 @@
 
 def grad_kernel(width, att, cot_t, lse, sums, grad_t, normed_t, stats, msg, far):
     whole = jnp.sum(sums[...], axis=0)
+    parts = {}
     for me in range(4):
         rms = lax.rsqrt(whole[2 * me : 2 * me + 1, :] / width + EPS)
         slope = rms * whole[2 * me + 1 : 2 * me + 2, :] / width
@@ -270,10 +280,14 @@
         deltas = [jnp.sum(product[feats(h)], axis=0, keepdims=True) for h in range(HEADS)]
         mine = stacked([lse[me, 0:HEADS, :]] + deltas)
         stats[me] = mine
-        at = STATS + 32 * (2 * side + block)
-        rows = stacked(split(mine) + (jnp.zeros_like(mine),)).astype(BF16)
-        msg[at : at + 32, :] = rows
-        far[at : at + 32, :] = rows
+        parts[2 * side + block] = split(mine)
+    rows = stacked(
+        [parts[at][0] for at in range(4)]
+        + [parts[at][1] for at in range(4)]
+        + [parts[at][2][0:HEADS] for at in range(4)]
+    ).astype(BF16)
+    msg[STATS:MSG2, :] = rows
+    far[STATS:MSG2, :] = rows
     far[MSG2:FAR2, :] = jnp.zeros((16, FEATS), BF16)
 
 
@@ -282,13 +296,12 @@
 
 
 def other_grads(msg, g_t, columns):
-    for side in range(2):
-        for block in range(2):
-            low = side * ROWS + block * BLOCK
-            g_t[side * 2 + block] = msg[low : low + BLOCK, :].T
-            low = STATS + 32 * (side * 2 + block)
-            rows = msg[low : low + 32, :].astype(F32)
-            columns[side * 2 + block] = as_columns(rows[0:8] + rows[8:16] + rows[16:24])
+    high = msg[STATS:MIDDLE, :].astype(F32) + msg[MIDDLE:LOW, :].astype(F32)
+    rest = msg[LOW:MSG2, :].astype(F32)
+    for at in range(4):
+        g_t[at] = msg[at * BLOCK : (at + 1) * BLOCK, :].T
+        whole = high[8 * at : 8 * at + 8]
+        columns[at] = as_columns(stacked([whole[0:HEADS] + rest[4 * at : 4 * at + 4], whole[HEADS : 2 * HEADS]]))
 
 
 def in_order(dots, weigh, outs):
@@ -313,7 +326,9 @@
     return slope.astype(BF16), self_p.astype(BF16), other_p.astype(BF16)
 
 
-def back(msg1, msg2, a_t, g_t, columns, self_a, self_v, self_g, stats, grad_a, grad_v, todo, count, first=0):
+def back(
+    msg1, msg2, a_t, g_t, columns, self_a, self_v, self_g, stats, grad_a, grad_v, todo, first, count, held=None
+):
     def pair(n, _):
         entry = todo[n]
         me = lax.div(entry, 2)
@@ -328,7 +343,7 @@
 
         def dots(h):
             made[h] = (
-                dot(msg1[pl.ds(row_a, BLOCK), lanes(h)], self_a[me, h]),
+                dot(msg1[pl.ds(row_a, BLOCK), lanes(h)], self_a[me, h]) if held is None else held[n, h],
                 dot(msg1[pl.ds(row_v, BLOCK), lanes(h)], self_g[me, h]),
                 dot(msg2[pl.ds(row_g, BLOCK), lanes(h)], self_v[me, h]),
             )
@@ -400,13 +415,12 @@
     lax.fori_loop(0, count, pair, 0)
 
 
-def back_own(msg1, msg2, columns, self_a, self_v, self_g, grad_t, stats, grad_a, grad_v, todo, count):
+def back_own(msg1, msg2, columns, self_a, self_v, self_g, grad_t, stats, held, grad_a, grad_v, todo, count):
     def pair(n, _):
         entry = todo[n]
         me = lax.div(entry, 2)
         block = lax.rem(entry, 2)
         frame = 2 + block
-        row_a = pl.multiple_of(KEYS + block * BLOCK, BLOCK)
         row_v = pl.multiple_of(FVALS + block * BLOCK, BLOCK)
         row_g = pl.multiple_of(block * BLOCK, BLOCK)
         mine, theirs = stats[me], columns[block]
@@ -414,7 +428,7 @@
 
         def dots(h):
             made[h] = (
-                dot(msg1[pl.ds(row_a, BLOCK), lanes(h)], self_a[me, h]),
+                held[n, h],
                 dot(msg1[pl.ds(row_v, BLOCK), lanes(h)], self_g[me, h]),
                 dot(msg2[pl.ds(row_g, BLOCK), lanes(h)], self_v[me, h]),
             )
@@ -443,7 +457,7 @@
 
 
 def own_backward(
-    plan, own1, own2, self_a, self_v, grad_t, stats, self_g, grad_a, grad_v, columns, todo
+    plan, own1, own2, self_a, self_v, grad_t, stats, own_scores, self_g, grad_a, grad_v, columns, todo
 ):
     for me in range(4):
         for h in range(HEADS):
@@ -453,16 +467,27 @@
     for block in range(2):
         columns[block] = as_columns(stats[2 + block])
     count = pair_list(todo, plan[0], jnp.int32(0))
-    back_own(own1, own2, columns, self_a, self_v, self_g, grad_t, stats, grad_a, grad_v, todo, count)
+    back_own(own1, own2, columns, self_a, self_v, self_g, grad_t, stats, own_scores, grad_a, grad_v, todo, count)
+
+
+def touched_blocks(as_events, as_frames):
+    return [jnp.bitwise_and(as_events, 3 * 4**a) != 0 for a in range(2)] + [
+        jnp.bitwise_and(as_frames, 5 * 2**f) != 0 for f in range(2)
+    ]
+
+
+def wait_grads(me, ready, outs, sems):
+    side, low = me // 2, (me % 2) * BLOCK
+    for k in range(2):
+        at = 2 * me + k
+        pltpu.make_async_copy(ready.at[at], outs[2 * side + k].at[low : low + BLOCK], sems.at[at]).wait()
 
 
 def send_grads(me, grad_a, grad_v, ready, outs, sems):
     side, low = me // 2, (me % 2) * BLOCK
-    copies = []
     for k, grad in enumerate((grad_a, grad_v)):
         ready[2 * me + k] = grad[me].astype(BF16).T
-        copies += start_all((ready.at[2 * me + k], outs[2 * side + k].at[low : low + BLOCK], sems.at[2 * me + k]))
-    return copies
+        start_all((ready.at[2 * me + k], outs[2 * side + k].at[low : low + BLOCK], sems.at[2 * me + k]))
 
 
 def near_backward(
@@ -476,6 +501,7 @@
     near_a_t,
     normed_t,
     stats,
+    near_scores,
     grad_a_in,
     grad_v_in,
     grad_a,
@@ -499,21 +525,35 @@
     grad_v[...] = grad_v_in[...]
     other_grads(near2, g_t, columns)
     count = pair_list(todo, plan[1], read_code(near1, 0))
-    back(near1, near2, near_a_t, g_t, columns, self_a, self_v, self_g, stats, grad_a, grad_v, todo, count)
+    known = near1, near2, near_a_t, g_t, columns, self_a, self_v, self_g, stats, grad_a, grad_v, todo
+    back(*known, 0, jnp.minimum(count, HELD), near_scores)
+    back(*known, HELD, count)
     outs = (grad_queries, grad_event_values, grad_keys, grad_frame_values)
+    code = read_code(far1, 1)
+    later = touched_blocks(plan[2], code)
     copies = []
     for me in range(4):
-        copies += send_grads(me, grad_a, grad_v, ready, outs, sems)
+
+        @pl.when(jnp.logical_not(later[me]))
+        def _():
+            send_grads(me, grad_a, grad_v, ready, outs, sems)
+
+    for me in range(4):
         low = (me % 2) * BLOCK
         ready[8 + me] = normed_t[me].T
         copies += start_all(
             (ready.at[8 + me], (event_out, frame_out)[me // 2].at[low : low + BLOCK], sems.at[8 + me])
         )
     other_queries(far1, far_a_t)
-    count = pair_list(todo, plan[2], read_code(far1, 1))
+    count = pair_list(todo, plan[2], code)
     part_way(far1, self_a, self_g, stats, kept_scores, kept_terms, todo, jnp.minimum(count, KEPT))
     for c in copies:
         c.wait()
+    for me in range(4):
+
+        @pl.when(jnp.logical_not(later[me]))
+        def _():
+            wait_grads(me, ready, outs, sems)
 
 
 def far_backward(
@@ -546,9 +586,7 @@
     sems,
 ):
     code = read_code(far1, 1)
-    touched = [jnp.bitwise_and(plan[2], 3 * 4**a) != 0 for a in range(2)] + [
-        jnp.bitwise_and(code, 5 * 2**f) != 0 for f in range(2)
-    ]
+    touched = touched_blocks(plan[2], code)
     outs = (grad_queries, grad_event_values, grad_keys, grad_frame_values)
     count = pair_list(todo, plan[2], code)
 
@@ -565,7 +603,7 @@
         begun = jnp.minimum(count, KEPT)
         back_rest(far2, far_a_t, g_t, columns, self_v, kept_scores, kept_terms, grad_a, grad_v, todo, begun)
         back(
-            far1, far2, far_a_t, g_t, columns, self_a, self_v, self_g, stats, grad_a, grad_v, todo, count, begun
+            far1, far2, far_a_t, g_t, columns, self_a, self_v, self_g, stats, grad_a, grad_v, todo, begun, count
         )
         for me in range(4):
 
@@ -577,11 +615,7 @@
 
             @pl.when(touched[me])
             def _():
-                side, low = me // 2, (me % 2) * BLOCK
-                for k in range(2):
-                    pltpu.make_async_copy(
-                        ready.at[2 * me + k], outs[2 * side + k].at[low : low + BLOCK], sems.at[2 * me + k]
-                    ).wait()
+                wait_grads(me, ready, outs, sems)
 
 
 def shape(*dims, dtype=F32):
@@ -642,7 +676,8 @@
     msg1 = far_msg1[0:MSG1]
     near1 = lax.ppermute(msg1, "st", inner_pairs)
 
-    self_a, self_v, cot_t, soft, acc, near_a_t = kernel(
+    held = shape(HELD + 1, HEADS, BLOCK, BLOCK)
+    self_a, self_v, cot_t, soft, acc, near_a_t, own_scores, near_scores = kernel(
         near_forward,
         (plan, msg1, near1, event_cotangent, frame_cotangent),
         "svvhh",
@@ -653,13 +688,14 @@
             shape(*small),
             shape(*tile),
             shape(*tile, dtype=BF16),
+            held,
+            held,
         ),
-        "vvvvvv",
+        "vvvvvvvv",
         [
             pltpu.VMEM((2, ROWS, FEATS), BF16),
             pltpu.VMEM(tile, BF16),
             pltpu.VMEM(tile, BF16),
-            pltpu.VMEM((HEADS, BLOCK, BLOCK), F32),
             todo,
             pltpu.SemaphoreType.DMA((2,)),
         ],
@@ -674,7 +710,7 @@
         [
             pltpu.VMEM(small, F32),
             pltpu.VMEM(tile, BF16),
-            pltpu.VMEM((HEADS, BLOCK, BLOCK), F32),
+            pltpu.VMEM((1, HEADS, BLOCK, BLOCK), F32),
             todo,
         ],
         1e6,
@@ -700,8 +736,8 @@
 
     self_g, grad_a, grad_v = kernel(
         own_backward,
-        (plan, msg1, msg2, self_a, self_v, grad_t, stats),
-        "svvvvvv",
+        (plan, msg1, msg2, self_a, self_v, grad_t, stats, own_scores),
+        "svvvvvvv",
         (shape(*wide, dtype=BF16), shape(*tile), shape(*tile)),
         "vvv",
         [pltpu.VMEM((2, BLOCK, PAIR), F32), todo],
@@ -710,8 +746,8 @@
     whole = [shape(ROWS, FEATS, dtype=BF16)]
     grad_a, grad_v, event_out, frame_out, *grads, far_a_t, kept_scores, kept_terms = kernel(
         near_backward,
-        (plan, near1, far1, near2, self_a, self_v, self_g, near_a_t, normed_t, stats, grad_a, grad_v),
-        "svvvvvvvvvvv",
+        (plan, near1, far1, near2, self_a, self_v, self_g, near_a_t, normed_t, stats, near_scores, grad_a, grad_v),
+        "svvvvvvvvvvvv",
         [shape(*tile)] * 2 + whole * 6 + [shape(*tile, dtype=BF16)] + [shape(KEPT, HEADS, BLOCK, BLOCK)] * 2,
         "vvhhhhhhvvv",
         [

time: 54.9 us -> 53.6 us (0.976)
  the two profiles are of different devices: /device:TPU:249 before, /device:TPU:185 now
where the time goes in v4:
time: 53.6 us; the launch traced here: 53.1 us
  Pallas kernels  23 us (43%)
  starting transfers between devices  12.8 us (24%)
  blocking collectives  8.11 us (15%)
  waiting for transfers between devices  6.42 us (12%)
  local copies, waits for them, and re-layouts  1.98 us (4%)
  between operations  0.75 us (1%)
    pallas_call x7, Pallas kernels, kernel(): pl.pallas_call(body, out_shape=tuple(outs), in_specs=specs(places), out_s...  23 us
    all_to_all x1, blocking collectives, on_device(): sums = lax.all_to_all(sums, 'hd', 0, 0)  8.11 us
    ppermute x1, starting transfers between devices, on_device(): far2 = lax.ppermute(far_msg2, 'st', outer_pairs)  5.18 us
    ppermute x1, waiting for transfers between devices, on_device(): far1 = lax.ppermute(far_msg1, 'st', outer_pairs)  3.77 us
    ppermute x1, starting transfers between devices, on_device(): far1 = lax.ppermute(far_msg1, 'st', outer_pairs)  3.76 us
    ppermute x1, waiting for transfers between devices, on_device(): near1 = lax.ppermute(msg1, 'st', inner_pairs)  2.64 us
    ppermute x1, starting transfers between devices, on_device(): near1 = lax.ppermute(msg1, 'st', inner_pairs)  1.92 us
    ppermute x1, starting transfers between devices, on_device(): near2 = lax.ppermute(msg2, 'st', inner_pairs)  1.92 us
  transfers between devices with their start and end apart: 4, of which 2 were waited for; matrix products, arithmetic and copies ran while one was open for 2% of the time, Pallas kernels for 23%

profile of v4, /device:TPU:185, one launch (start us, length us, event | category | flops | bytes accessed | tf_op | source)
XLA Modules:
  0.0 53.1 jit_solution(16773642303669770515)
XLA Ops:
  0.6 0.0 copy-start.1
  0.6 0.0 copy-start
  0.7 2.3 %shard_map.127 = (bf16[2080,256]{1,0:T(8,128)(2,1)}, s32[8]{0:T(128)}) custom-call(s32[2,3]{1,0:T(2,128)} %partner_in.1, s32[2]{0:T(128)} %live_in.1, bf16[512,256]{1,0:T(8,128)(2,1)} %queries.1, bf16[512,256]{1,0:T(8,128)(2,1)} %event_values.1, bf16[512,256]{1,0:T(8,128)(2,1)} %keys.1, bf16[512,256]{1,0:T(8,128)(2,1)} %frame_values.1), custom_call_target="tpu_custom_call" | custom-call | bytes 1024 | tf_op jit(solution)/shard_map/pallas_call | solution.py:631
  3.0 0.0 copy-start.3
  3.0 3.8 %collective-permute-start.1 = (bf16[2080,256]{1,0:T(8,128)(2,1)}, bf16[2080,256]{1,0:T(8,128)(2,1)S(1)}, u32[]{:S(2)}, u32[]{:S(2)}) collective-permute-start(bf16[2080,256]{1,0:T(8,128)(2,1)} %get-tuple-element.43), channel_id=1, source_target_pairs={{4,8},{12,16},{20,24},{28,32},{36,40},{44,48},{52,56},{60,64},{68,... | collective-permute-start | bytes 3194888 | tf_op jit(solution)/shard_map/ppermute | solution.py:675
  6.7 1.3 %slice.3.own.own1 = bf16[2064,256]{1,0:T(8,128)(2,1)S(1)} slice(bf16[2080,256]{1,0:T(8,128)(2,1)} %get-tuple-element.43), slice={[0:2064], [0:256]} | slice | bytes 2113536 | tf_op jit(solution)/shard_map/slice | solution.py:676
  8.0 1.9 %collective-permute-start = (bf16[2064,256]{1,0:T(8,128)(2,1)S(1)}, bf16[2064,256]{1,0:T(8,128)(2,1)S(1)}, u32[]{:S(2)}, u32[]{:S(2)}) collective-permute-start(bf16[2064,256]{1,0:T(8,128)(2,1)S(1)} %slice.3.own.own1), channel_id=1, source_target_pairs={{0,4},{4,0},{8,12},{12,8},{16,20},{20,16},{24,28},{28,24},{32,36},... | collective-permute-start | bytes 3170312 | tf_op jit(solution)/shard_map/ppermute | solution.py:677
  10.0 2.6 %collective-permute-done.near.near1 = bf16[2064,256]{1,0:T(8,128)(2,1)S(1)} collective-permute-done((bf16[2064,256]{1,0:T(8,128)(2,1)S(1)}, bf16[2064,256]{1,0:T(8,128)(2,1)S(1)}, u32[]{:S(2)}, u32[]{:S(2)}) %collective-permute-start) | collective-permute-done | bytes 1056800 | tf_op jit(solution)/shard_map/ppermute | solution.py:677
  12.6 0.0 copy-done.1
  12.6 0.0 copy-done
  12.6 0.0 copy-start.2
  12.6 0.7 %copy-done.2 = s32[8]{0:T(128)S(1)} copy-done((s32[8]{0:T(128)S(1)}, s32[8]{0:T(128)}, u32[]{:S(2)}) %copy-start.2) | copy-done | bytes 56
  13.3 4.5 %shard_map.128 = (bf16[4,4,128,256]{3,2,1,0:T(8,128)(2,1)S(1)}, bf16[4,4,128,256]{3,2,1,0:T(8,128)(2,1)S(1)}, bf16[4,256,256]{2,1,0:T(8,128)(2,1)S(1)}, f32[4,8,...) custom-call(s32[8]{0:T(128)S(1)} %copy-done.2, ...), custom_call_target="tpu_custom_call" | custom-call | flops 1000000 | bytes 1024 | tf_op jit(solution)/shard_map/pallas_call | solution.py:631
  17.8 3.8 %collective-permute-done.1.far.far1 = bf16[2080,256]{1,0:T(8,128)(2,1)S(1)} collective-permute-done((bf16[2080,256]{1,0:T(8,128)(2,1)}, bf16[2080,256]{1,0:T(8,128)(2,1)S(1)}, u32[]{:S(2)}, u32[]{:S(2)}) %collective-permute-start.1) | collective-permute-done | bytes 1064992 | tf_op jit(solution)/shard_map/ppermute | solution.py:675
  21.6 0.0 copy-done.3
  21.6 3.0 %shard_map.129 = (f32[4,256,256]{2,1,0:T(8,128)S(1)}, f32[4,8,256]{2,1,0:T(8,128)S(1)}, f32[4,8,256]{2,1,0:T(8,128)S(1)}) custom-call(s32[8]{0:T(128)S(1)} %copy-done.3, bf16[2080,256]{1,0:T(8,128)(2,1)S(1)} %collective-permute-done.1.far.far1, bf16[4,4,128,256]{3,2,1,0:T(8,128)(2,1)S(1)} %get-tuple-element.44.self_a, ...), custom_call_target="tpu_custom_call" | custom-call | flops 1000000 | bytes 1024 | tf_op jit(solution)/shard_map/pallas_call | solution.py:631
  24.6 8.1 %all_to_all.5.refs_3_ = f32[4,8,256]{2,1,0:T(8,128)S(1)} all-to-all(f32[4,8,256]{2,1,0:T(8,128)S(1)} %get-tuple-element.50), channel_id=1, replica_groups=mesh['st'=128,'hd'=4] {'hd'}, dimensions={0} | all-to-all | bytes 65536 | tf_op jit(solution)/shard_map/all_to_all | solution.py:718
  32.7 0.4 shard_map.130
  33.1 5.2 %collective-permute-start.3 = (bf16[1120,256]{1,0:T(8,128)(2,1)S(1)}, bf16[1120,256]{1,0:T(8,128)(2,1)S(1)}, u32[]{:S(2)}, u32[]{:S(2)}) collective-permute-start(bf16[1120,256]{1,0:T(8,128)(2,1)S(1)} %get-tuple-element.64), channel_id=1, source_target_pairs={{4,8},{12,16},{20,24},{28,32},{36,40},{44,48},{52,56},{60,64},{68,... | collective-permute-start | bytes 1720328 | tf_op jit(solution)/shard_map/ppermute | solution.py:734
  38.3 1.9 %collective-permute-start.2 = (bf16[1104,256]{1,0:T(8,128)(2,1)S(1)}, bf16[1104,256]{1,0:T(8,128)(2,1)S(1)}, u32[]{:S(2)}, u32[]{:S(2)}) collective-permute-start(bf16[1104,256]{1,0:T(8,128)(2,1)S(1)} %get-tuple-element.51.own2), channel_id=1, source_target_pairs={{0,4},{4,0},{8,12},{12,8},{16,20},{20,16},{24,28},{28,24},{32,36},... | collective-permute-start | bytes 1695752 | tf_op jit(solution)/shard_map/ppermute | solution.py:735
  40.2 3.0 %shard_map.131 = (bf16[4,4,128,256]{3,2,1,0:T(8,128)(2,1)S(1)}, f32[4,256,256]{2,1,0:T(8,128)S(1)}, f32[4,256,256]{2,1,0:T(8,128)S(1)}) custom-call(s32[8]{0:T(128)S(1)} %copy-done.3, bf16[2064,256]{1,0:T(8,128)(2,1)S(1)} %slice.3.own.own1, bf16[1104,256]{1,0:T(8,128)(2,1)S(1)} %get-tuple-element.51.own2, ...), custom_call_target="tpu_custom_call" | custom-call | flops 1000000 | bytes 1024 | tf_op jit(solution)/shard_map/pallas_call | solution.py:631
  43.3 0.0 collective-permute-done.2.near2
  43.3 4.6 %shard_map.132 = (f32[4,256,256]{2,1,0:T(8,128)S(1)}, f32[4,256,256]{2,1,0:T(8,128)S(1)}, bf16[512,256]{1,0:T(8,128)(2,1)}, bf16[512,256]{1,0:T(8,128)(2,1)}, bf...) custom-call(s32[8]{0:T(128)S(1)} %copy-done.3, ...), custom_call_target="tpu_custom_call" | custom-call | flops 1000000 | bytes 1024 | tf_op jit(solution)/shard_map/pallas_call | solution.py:631
  47.9 0.0 collective-permute-done.3.far2
  47.9 5.1 %shard_map.133 = (bf16[512,256]{1,0:T(8,128)(2,1)}, bf16[512,256]{1,0:T(8,128)(2,1)}, bf16[512,256]{1,0:T(8,128)(2,1)}, bf16[512,256]{1,0:T(8,128)(2,1)}) custom-call(s32[8]{0:T(128)S(1)} %copy-done.3, bf16[2080,256]{1,0:T(8,128)(2,1)S(1)} %collective-permute-done.1.far.far1, ...), custom_call_target="tpu_custom_call", output_to_operand_aliasing={{0}: (12, {}), {1}: (13, {}), {2}: (14, {}), {3}: (15, {})} | custom-call | flops 1000000 | bytes 1024 | tf_op jit(solution)/shard_map/pallas_call | solution.py:631
Async XLA Ops:
  0.6 12.0 %copy-start.1 = (bf16[512,256]{1,0:T(8,128)(2,1)S(1)}, bf16[512,256]{1,0:T(8,128)(2,1)}, u32[]{:S(2)}) copy-start(bf16[512,256]{1,0:T(8,128)(2,1)} %frame_cot.1) | copy-start | bytes 786436
  0.6 12.0 %copy-start = (bf16[512,256]{1,0:T(8,128)(2,1)S(1)}, bf16[512,256]{1,0:T(8,128)(2,1)}, u32[]{:S(2)}) copy-start(bf16[512,256]{1,0:T(8,128)(2,1)} %event_cot.1) | copy-start | bytes 786436
  3.0 18.6 %copy-start.3 = (s32[8]{0:T(128)S(1)}, s32[8]{0:T(128)}, u32[]{:S(2)}) copy-start(s32[8]{0:T(128)} %get-tuple-element.42.plan) | copy-start | bytes 100
  3.0 18.6 %collective-permute-start.1 = (bf16[2080,256]{1,0:T(8,128)(2,1)}, bf16[2080,256]{1,0:T(8,128)(2,1)S(1)}, u32[]{:S(2)}, u32[]{:S(2)}) collective-permute-start(bf16[2080,256]{1,0:T(8,128)(2,1)} %get-tuple-element.43), channel_id=1, source_target_pairs={{4,8},{12,16},{20,24},{28,32},{36,40},{44,48},{52,56},{60,64},{68,... | collective-permute-start | bytes 3194888 | tf_op jit(solution)/shard_map/ppermute | solution.py:675
  8.0 4.6 %collective-permute-start = (bf16[2064,256]{1,0:T(8,128)(2,1)S(1)}, bf16[2064,256]{1,0:T(8,128)(2,1)S(1)}, u32[]{:S(2)}, u32[]{:S(2)}) collective-permute-start(bf16[2064,256]{1,0:T(8,128)(2,1)S(1)} %slice.3.own.own1), channel_id=1, source_target_pairs={{0,4},{4,0},{8,12},{12,8},{16,20},{20,16},{24,28},{28,24},{32,36},... | collective-permute-start | bytes 3170312 | tf_op jit(solution)/shard_map/ppermute | solution.py:677
  12.6 0.7 %copy-start.2 = (s32[8]{0:T(128)S(1)}, s32[8]{0:T(128)}, u32[]{:S(2)}) copy-start(s32[8]{0:T(128)} %get-tuple-element.42.plan) | copy-start | bytes 100
  33.1 14.8 %collective-permute-start.3 = (bf16[1120,256]{1,0:T(8,128)(2,1)S(1)}, bf16[1120,256]{1,0:T(8,128)(2,1)S(1)}, u32[]{:S(2)}, u32[]{:S(2)}) collective-permute-start(bf16[1120,256]{1,0:T(8,128)(2,1)S(1)} %get-tuple-element.64), channel_id=1, source_target_pairs={{4,8},{12,16},{20,24},{28,32},{36,40},{44,48},{52,56},{60,64},{68,... | collective-permute-start | bytes 1720328 | tf_op jit(solution)/shard_map/ppermute | solution.py:734
  38.3 5.0 %collective-permute-start.2 = (bf16[1104,256]{1,0:T(8,128)(2,1)S(1)}, bf16[1104,256]{1,0:T(8,128)(2,1)S(1)}, u32[]{:S(2)}, u32[]{:S(2)}) collective-permute-start(bf16[1104,256]{1,0:T(8,128)(2,1)S(1)} %get-tuple-element.51.own2), channel_id=1, source_target_pairs={{0,4},{4,0},{8,12},{12,8},{16,20},{20,16},{24,28},{28,24},{32,36},... | collective-permute-start | bytes 1695752 | tf_op jit(solution)/shard_map/ppermute | solution.py:735

commit v5 on v4

--- a/solution.py
+++ b/solution.py
@@ -143,15 +143,17 @@
         for h in range(HEADS):
             ahead[slot, h] = scores[h]
 
-    keep(0, scores_of(0))
-
-    def pair(n, _):
+    @pl.when(count > 0)
+    def _():
+        keep(0, scores_of(0))
+
+    def add(n, last):
         me, at, _ = place(n)
         old, whole = soft[me], acc[me]
         slot = jnp.minimum(n, slots - 1)
         scores = [ahead[slot, h] for h in range(HEADS)]
-        after = jnp.minimum(n + 1, count - 1)
-        following = scores_of(after)
+        if not last:
+            following = scores_of(n + 1)
         tops, totals, decays, weights = [], [], [], []
         for h in range(HEADS):
             top = jnp.maximum(old[h : h + 1], jnp.max(scores[h], axis=0, keepdims=True))
@@ -165,10 +167,18 @@
             [whole[feats(h)] * decays[h] + dot(vals_t[at, feats(h), :], weights[h]) for h in range(HEADS)]
         )
         soft[me] = stacked(tops + totals)
-        keep(after, following)
+        if not last:
+            keep(n + 1, following)
+
+    def pair(n, _):
+        add(n, False)
         return 0
 
-    lax.fori_loop(0, count, pair, 0)
+    lax.fori_loop(0, count - 1, pair, 0)
+
+    @pl.when(count > 0)
+    def _():
+        add(count - 1, True)
 
 
 def other_values(msg, vals_t):

time: 53.6 us -> 54.8 us (1.022)
  the two profiles are of different devices: /device:TPU:185 before, /device:TPU:384 now
where the time goes in v5:
time: 54.8 us; the launch traced here: 54.5 us
  Pallas kernels  26.3 us (48%)
  starting transfers between devices  12 us (22%)
  blocking collectives  9.53 us (17%)
  waiting for transfers between devices  3.99 us (7%)
  local copies, waits for them, and re-layouts  1.98 us (4%)
  between operations  0.75 us (1%)
    pallas_call x7, Pallas kernels, kernel(): pl.pallas_call(body, out_shape=tuple(outs), in_specs=specs(places), out_s...  26.3 us
    all_to_all x1, blocking collectives, on_device(): sums = lax.all_to_all(sums, 'hd', 0, 0)  9.53 us
    ppermute x1, starting transfers between devices, on_device(): far1 = lax.ppermute(far_msg1, 'st', outer_pairs)  4.81 us
    ppermute x1, starting transfers between devices, on_device(): far2 = lax.ppermute(far_msg2, 'st', outer_pairs)  3.37 us
    ppermute x1, waiting for transfers between devices, on_device(): near1 = lax.ppermute(msg1, 'st', inner_pairs)  2.64 us
    ppermute x1, starting transfers between devices, on_device(): near1 = lax.ppermute(msg1, 'st', inner_pairs)  1.92 us
    ppermute x1, starting transfers between devices, on_device(): near2 = lax.ppermute(msg2, 'st', inner_pairs)  1.92 us
    ppermute x1, waiting for transfers between devices, on_device(): far1 = lax.ppermute(far_msg1, 'st', outer_pairs)  1.34 us
  transfers between devices with their start and end apart: 4, of which 2 were waited for; matrix products, arithmetic and copies ran while one was open for 2% of the time, Pallas kernels for 28%

profile of v5, /device:TPU:384, one launch (start us, length us, event | category | flops | bytes accessed | tf_op | source)
XLA Modules:
  0.0 54.5 jit_solution(10645209050855981238)
XLA Ops:
  0.6 0.0 copy-start.1
  0.6 0.0 copy-start
  0.7 2.3 %shard_map.127 = (bf16[2080,256]{1,0:T(8,128)(2,1)}, s32[8]{0:T(128)}) custom-call(s32[2,3]{1,0:T(2,128)} %partner_in.1, s32[2]{0:T(128)} %live_in.1, bf16[512,256]{1,0:T(8,128)(2,1)} %queries.1, bf16[512,256]{1,0:T(8,128)(2,1)} %event_values.1, bf16[512,256]{1,0:T(8,128)(2,1)} %keys.1, bf16[512,256]{1,0:T(8,128)(2,1)} %frame_values.1), custom_call_target="tpu_custom_call" | custom-call | bytes 1024 | tf_op jit(solution)/shard_map/pallas_call | solution.py:641
  3.0 0.0 copy-start.3
  3.0 4.8 %collective-permute-start.1 = (bf16[2080,256]{1,0:T(8,128)(2,1)}, bf16[2080,256]{1,0:T(8,128)(2,1)S(1)}, u32[]{:S(2)}, u32[]{:S(2)}) collective-permute-start(bf16[2080,256]{1,0:T(8,128)(2,1)} %get-tuple-element.43), channel_id=1, source_target_pairs={{4,8},{12,16},{20,24},{28,32},{36,40},{44,48},{52,56},{60,64},{68,... | collective-permute-start | bytes 3194888 | tf_op jit(solution)/shard_map/ppermute | solution.py:685
  7.8 1.3 %slice.3.own.own1 = bf16[2064,256]{1,0:T(8,128)(2,1)S(1)} slice(bf16[2080,256]{1,0:T(8,128)(2,1)} %get-tuple-element.43), slice={[0:2064], [0:256]} | slice | bytes 2113536 | tf_op jit(solution)/shard_map/slice | solution.py:686
  9.1 1.9 %collective-permute-start = (bf16[2064,256]{1,0:T(8,128)(2,1)S(1)}, bf16[2064,256]{1,0:T(8,128)(2,1)S(1)}, u32[]{:S(2)}, u32[]{:S(2)}) collective-permute-start(bf16[2064,256]{1,0:T(8,128)(2,1)S(1)} %slice.3.own.own1), channel_id=1, source_target_pairs={{0,4},{4,0},{8,12},{12,8},{16,20},{20,16},{24,28},{28,24},{32,36},... | collective-permute-start | bytes 3170312 | tf_op jit(solution)/shard_map/ppermute | solution.py:687
  11.0 2.6 %collective-permute-done.near.near1 = bf16[2064,256]{1,0:T(8,128)(2,1)S(1)} collective-permute-done((bf16[2064,256]{1,0:T(8,128)(2,1)S(1)}, bf16[2064,256]{1,0:T(8,128)(2,1)S(1)}, u32[]{:S(2)}, u32[]{:S(2)}) %collective-permute-start) | collective-permute-done | bytes 1056800 | tf_op jit(solution)/shard_map/ppermute | solution.py:687
  13.7 0.0 copy-done.1
  13.7 0.0 copy-done
  13.7 0.0 copy-start.2
  13.7 0.7 %copy-done.2 = s32[8]{0:T(128)S(1)} copy-done((s32[8]{0:T(128)S(1)}, s32[8]{0:T(128)}, u32[]{:S(2)}) %copy-start.2) | copy-done | bytes 56
  14.3 5.9 %shard_map.128 = (bf16[4,4,128,256]{3,2,1,0:T(8,128)(2,1)S(1)}, bf16[4,4,128,256]{3,2,1,0:T(8,128)(2,1)S(1)}, bf16[4,256,256]{2,1,0:T(8,128)(2,1)S(1)}, f32[4,8,...) custom-call(s32[8]{0:T(128)S(1)} %copy-done.2, ...), custom_call_target="tpu_custom_call" | custom-call | flops 1000000 | bytes 1024 | tf_op jit(solution)/shard_map/pallas_call | solution.py:641
  20.2 1.3 %collective-permute-done.1.far.far1 = bf16[2080,256]{1,0:T(8,128)(2,1)S(1)} collective-permute-done((bf16[2080,256]{1,0:T(8,128)(2,1)}, bf16[2080,256]{1,0:T(8,128)(2,1)S(1)}, u32[]{:S(2)}, u32[]{:S(2)}) %collective-permute-start.1) | collective-permute-done | bytes 1064992 | tf_op jit(solution)/shard_map/ppermute | solution.py:685
  21.6 0.0 copy-done.3
  21.6 3.0 %shard_map.129 = (f32[4,256,256]{2,1,0:T(8,128)S(1)}, f32[4,8,256]{2,1,0:T(8,128)S(1)}, f32[4,8,256]{2,1,0:T(8,128)S(1)}) custom-call(s32[8]{0:T(128)S(1)} %copy-done.3, bf16[2080,256]{1,0:T(8,128)(2,1)S(1)} %collective-permute-done.1.far.far1, bf16[4,4,128,256]{3,2,1,0:T(8,128)(2,1)S(1)} %get-tuple-element.44.self_a, ...), custom_call_target="tpu_custom_call" | custom-call | flops 1000000 | bytes 1024 | tf_op jit(solution)/shard_map/pallas_call | solution.py:641
  24.6 9.5 %all_to_all.5.refs_3_ = f32[4,8,256]{2,1,0:T(8,128)S(1)} all-to-all(f32[4,8,256]{2,1,0:T(8,128)S(1)} %get-tuple-element.50), channel_id=1, replica_groups=mesh['st'=128,'hd'=4] {'hd'}, dimensions={0} | all-to-all | bytes 65536 | tf_op jit(solution)/shard_map/all_to_all | solution.py:728
  34.1 0.4 shard_map.130
  34.6 3.4 %collective-permute-start.3 = (bf16[1120,256]{1,0:T(8,128)(2,1)S(1)}, bf16[1120,256]{1,0:T(8,128)(2,1)S(1)}, u32[]{:S(2)}, u32[]{:S(2)}) collective-permute-start(bf16[1120,256]{1,0:T(8,128)(2,1)S(1)} %get-tuple-element.64), channel_id=1, source_target_pairs={{4,8},{12,16},{20,24},{28,32},{36,40},{44,48},{52,56},{60,64},{68,... | collective-permute-start | bytes 1720328 | tf_op jit(solution)/shard_map/ppermute | solution.py:744
  37.9 1.9 %collective-permute-start.2 = (bf16[1104,256]{1,0:T(8,128)(2,1)S(1)}, bf16[1104,256]{1,0:T(8,128)(2,1)S(1)}, u32[]{:S(2)}, u32[]{:S(2)}) collective-permute-start(bf16[1104,256]{1,0:T(8,128)(2,1)S(1)} %get-tuple-element.51.own2), channel_id=1, source_target_pairs={{0,4},{4,0},{8,12},{12,8},{16,20},{20,16},{24,28},{28,24},{32,36},... | collective-permute-start | bytes 1695752 | tf_op jit(solution)/shard_map/ppermute | solution.py:745
  39.9 4.1 %shard_map.131 = (bf16[4,4,128,256]{3,2,1,0:T(8,128)(2,1)S(1)}, f32[4,256,256]{2,1,0:T(8,128)S(1)}, f32[4,256,256]{2,1,0:T(8,128)S(1)}) custom-call(s32[8]{0:T(128)S(1)} %copy-done.3, bf16[2064,256]{1,0:T(8,128)(2,1)S(1)} %slice.3.own.own1, bf16[1104,256]{1,0:T(8,128)(2,1)S(1)} %get-tuple-element.51.own2, ...), custom_call_target="tpu_custom_call" | custom-call | flops 1000000 | bytes 1024 | tf_op jit(solution)/shard_map/pallas_call | solution.py:641
  44.0 0.0 collective-permute-done.2.near2
  44.0 5.4 %shard_map.132 = (f32[4,256,256]{2,1,0:T(8,128)S(1)}, f32[4,256,256]{2,1,0:T(8,128)S(1)}, bf16[512,256]{1,0:T(8,128)(2,1)}, bf16[512,256]{1,0:T(8,128)(2,1)}, bf...) custom-call(s32[8]{0:T(128)S(1)} %copy-done.3, ...), custom_call_target="tpu_custom_call" | custom-call | flops 1000000 | bytes 1024 | tf_op jit(solution)/shard_map/pallas_call | solution.py:641
  49.4 0.0 collective-permute-done.3.far2
  49.4 5.1 %shard_map.133 = (bf16[512,256]{1,0:T(8,128)(2,1)}, bf16[512,256]{1,0:T(8,128)(2,1)}, bf16[512,256]{1,0:T(8,128)(2,1)}, bf16[512,256]{1,0:T(8,128)(2,1)}) custom-call(s32[8]{0:T(128)S(1)} %copy-done.3, bf16[2080,256]{1,0:T(8,128)(2,1)S(1)} %collective-permute-done.1.far.far1, ...), custom_call_target="tpu_custom_call", output_to_operand_aliasing={{0}: (12, {}), {1}: (13, {}), {2}: (14, {}), {3}: (15, {})} | custom-call | flops 1000000 | bytes 1024 | tf_op jit(solution)/shard_map/pallas_call | solution.py:641
Async XLA Ops:
  0.6 13.0 %copy-start.1 = (bf16[512,256]{1,0:T(8,128)(2,1)S(1)}, bf16[512,256]{1,0:T(8,128)(2,1)}, u32[]{:S(2)}) copy-start(bf16[512,256]{1,0:T(8,128)(2,1)} %frame_cot.1) | copy-start | bytes 786436
  0.6 13.0 %copy-start = (bf16[512,256]{1,0:T(8,128)(2,1)S(1)}, bf16[512,256]{1,0:T(8,128)(2,1)}, u32[]{:S(2)}) copy-start(bf16[512,256]{1,0:T(8,128)(2,1)} %event_cot.1) | copy-start | bytes 786436
  3.0 18.6 %copy-start.3 = (s32[8]{0:T(128)S(1)}, s32[8]{0:T(128)}, u32[]{:S(2)}) copy-start(s32[8]{0:T(128)} %get-tuple-element.42.plan) | copy-start | bytes 100
  3.0 18.6 %collective-permute-start.1 = (bf16[2080,256]{1,0:T(8,128)(2,1)}, bf16[2080,256]{1,0:T(8,128)(2,1)S(1)}, u32[]{:S(2)}, u32[]{:S(2)}) collective-permute-start(bf16[2080,256]{1,0:T(8,128)(2,1)} %get-tuple-element.43), channel_id=1, source_target_pairs={{4,8},{12,16},{20,24},{28,32},{36,40},{44,48},{52,56},{60,64},{68,... | collective-permute-start | bytes 3194888 | tf_op jit(solution)/shard_map/ppermute | solution.py:685
  9.1 4.6 %collective-permute-start = (bf16[2064,256]{1,0:T(8,128)(2,1)S(1)}, bf16[2064,256]{1,0:T(8,128)(2,1)S(1)}, u32[]{:S(2)}, u32[]{:S(2)}) collective-permute-start(bf16[2064,256]{1,0:T(8,128)(2,1)S(1)} %slice.3.own.own1), channel_id=1, source_target_pairs={{0,4},{4,0},{8,12},{12,8},{16,20},{20,16},{24,28},{28,24},{32,36},... | collective-permute-start | bytes 3170312 | tf_op jit(solution)/shard_map/ppermute | solution.py:687
  13.7 0.7 %copy-start.2 = (s32[8]{0:T(128)S(1)}, s32[8]{0:T(128)}, u32[]{:S(2)}) copy-start(s32[8]{0:T(128)} %get-tuple-element.42.plan) | copy-start | bytes 100
  34.6 14.8 %collective-permute-start.3 = (bf16[1120,256]{1,0:T(8,128)(2,1)S(1)}, bf16[1120,256]{1,0:T(8,128)(2,1)S(1)}, u32[]{:S(2)}, u32[]{:S(2)}) collective-permute-start(bf16[1120,256]{1,0:T(8,128)(2,1)S(1)} %get-tuple-element.64), channel_id=1, source_target_pairs={{4,8},{12,16},{20,24},{28,32},{36,40},{44,48},{52,56},{60,64},{68,... | collective-permute-start | bytes 1720328 | tf_op jit(solution)/shard_map/ppermute | solution.py:744
  37.9 6.1 %collective-permute-start.2 = (bf16[1104,256]{1,0:T(8,128)(2,1)S(1)}, bf16[1104,256]{1,0:T(8,128)(2,1)S(1)}, u32[]{:S(2)}, u32[]{:S(2)}) collective-permute-start(bf16[1104,256]{1,0:T(8,128)(2,1)S(1)} %get-tuple-element.51.own2), channel_id=1, source_target_pairs={{0,4},{4,0},{8,12},{12,8},{16,20},{20,16},{24,28},{28,24},{32,36},... | collective-permute-start | bytes 1695752 | tf_op jit(solution)/shard_map/ppermute | solution.py:745
